TPU v7x, 256 devices: a whole 4x4x8 slice. The times are simulated.
256 devices in a mesh: seq: 16 (over y, x), tp: 8 (over z), tea: 2 (over core).
Axes of the slice: x: 4, y: 4, z: 8, core: 2. Of those that a mesh axis runs over, the one named last changes fastest.
Arguments:
- hidden_states: bfloat16 [12288, 3072], P(('seq', 'tea')), may hold values from -6 to 6
- w_in: bfloat16 [3072, 2048], P(None, 'tp'), may hold values from -0.109375 to 0.109375
- w_out: bfloat16 [2048, 1408], P('tp'), may hold values from -0.125 to 0.125
- teacher: bfloat16 [6144, 1408], P(('seq', 'tea')), may hold values from -6 to 6
- patch_map: int32 [12288], P(('seq', 'tea')), may hold values from 0 to 6143, as said below
- row_pick: int32 [16, 8, 2, 16], P('seq', 'tp', 'tea'), may hold values from 0 to 2
- key_pick: int32 [16, 8, 2, 16], P(None, 'tp', 'tea'), may hold values from 0 to 2
Outputs:
- grad_hidden: float32 [12288, 3072], P(('seq', 'tea'), 'tp')
- grad_w_in: float32 [3072, 2048], P(None, 'tp')
- grad_w_out: float32 [2048, 1408], P('tp')
Inputs may be any that keep to these rules, and one draw needn't show every extreme that they name: `patch_map`: the tokens of group q (rows q * 384 onward) name teacher rows q * 192 to (q + 1) * 192 - 1 only, each of them exactly 384 / 192 times.
All inputs are finite; a program needn't handle non-finite values.
Results may differ from a plain program's by a relative error of at most 0.0055.
Values may be sent and summed in bfloat16 or wider, within the bound.
No kernel may reach another device: no remote copies, remote signals or barrier semaphores. Data moves between devices by JAX's collectives and lax.ppermute only.
A program may use at most 128 MiB of HBM per device.

v0:
```python
import jax
import jax.numpy as jnp
from jax import lax
from jax.experimental import pallas as pl
from jax.experimental.pallas import tpu as pltpu
from jax.sharding import PartitionSpec as P

E = 1408
BLK = 128
RB = 3
SIDE = 4
NT = 8
GROUPS = SIDE * SIDE
SHARD = 48
ROWS = 384
E_WIDE = 1536
E_PAD = 1536

eps = 1e-06
bf16 = jnp.bfloat16
f32 = jnp.float32


def shift_tp(x, step):
    return lax.ppermute(x, "tp", [(i, (i + step) % NT) for i in range(NT)])


def swap_tea(x):
    return lax.ppermute(x, "tea", [(0, 1), (1, 0)])


LEFT = 768
RIGHT = 640


def gather_ring(x):
    before, after = shift_tp(x, 1), shift_tp(x, -1)
    before2, after2 = shift_tp(x, 2), shift_tp(x, -2)
    far_after = shift_tp(jnp.concatenate([after, after2[:, LEFT:]], axis=1), -2)
    far_before = shift_tp(jnp.concatenate([before, before2[:, :LEFT]], axis=1), 2)
    return [x, after, after2, far_after, before2, before, far_before]


def sum_ring(own, one, two, far_after, six, seven, far_before):
    far_after, far_before = shift_tp(far_after, 2).astype(f32), shift_tp(far_before, -2).astype(f32)
    one, seven = one + far_after[:, :E], seven + far_before[:, :E]
    two = two + jnp.concatenate([far_after[:, E:], jnp.zeros((SHARD, RIGHT), f32)], axis=1)
    six = six + jnp.concatenate([jnp.zeros((SHARD, LEFT), f32), far_before[:, E:]], axis=1)
    one, two, six, seven = (v.astype(bf16) for v in (one, two, six, seven))
    return [shift_tp(two, 2), shift_tp(six, -2), shift_tp(one, 1), shift_tp(seven, -1)]


def gather_split(x):
    before, after = shift_tp(x, 1), shift_tp(x, -1)
    before2, after2 = shift_tp(x, 2), shift_tp(x, -2)
    before3, after3 = shift_tp(before2, 1), shift_tp(after2, -1)
    left, right = shift_tp(before2[:, :LEFT], 2), shift_tp(after2[:, LEFT:], -2)
    return [x, after, after2, after3, left, right, before3, before2, before]


def pass_split(own, one, two, three, left, right, five, six, seven):
    three, five = shift_tp(three, 1), shift_tp(five, -1)
    left, right = shift_tp(left, 2), shift_tp(right, -2)
    one, seven = shift_tp(one, 1), shift_tp(seven, -1)
    blank = jnp.zeros(left.shape, f32), jnp.zeros(right.shape, f32)
    two = two + three.astype(f32) + jnp.concatenate([left.astype(f32), blank[1]], axis=1)
    six = six + five.astype(f32) + jnp.concatenate([blank[0], right.astype(f32)], axis=1)
    return one, seven, two.astype(bf16), six.astype(bf16)


def sum_split(*terms):
    one, seven, two, six = pass_split(*terms)
    return [one, seven, shift_tp(two, 2), shift_tp(six, -2)]


def to_all(x):
    return lax.all_to_all(jnp.broadcast_to(x[None], (GROUPS,) + x.shape), "seq", 0, 0, tiled=True)


def in_vmem(count):
    return [pl.BlockSpec(memory_space=pltpu.VMEM)] * count


def in_place(count):
    return [pl.BlockSpec(memory_space=pltpu.HBM)] * count


def hbm(x):
    return pltpu.with_memory_space_constraint(x, pltpu.HBM)


IN_SMEM = pl.BlockSpec(memory_space=pltpu.SMEM)
def scoped(mib):
    return pltpu.CompilerParams(vmem_limit_bytes=mib * 1024 * 1024)


PIECE_ORDER = (0, 1, 5, 2, 4, 3, 6)


def spot_of(at, d):
    return pl.multiple_of(lax.rem(at + d, NT) * SHARD, SHARD)


PARTS = 7
PLACES = (0, 1, 2, 3, 6, 7, 5)
STAGE = [pltpu.VMEM((5, SHARD, E), bf16), pltpu.SemaphoreType.DMA((NT + 1,))]
WIDE, FULL = pltpu.HBM((SHARD, E), f32), pltpu.HBM((SHARD, E), bf16)
SPLIT = [WIDE, FULL, WIDE, FULL, pltpu.HBM((SHARD, LEFT), bf16), pltpu.HBM((SHARD, RIGHT), bf16), FULL, WIDE, FULL]
CHUNKS = [
    WIDE,
    WIDE,
    WIDE,
    pltpu.HBM((SHARD, E + LEFT), bf16),
    WIDE,
    WIDE,
    pltpu.HBM((SHARD, E + RIGHT), bf16),
]


def far_parts(total_ref, at, after_ref, before_ref):
    half = total_ref[pl.ds(spot_of(at, 4), SHARD), :].astype(bf16)
    after_ref[:, :E] = total_ref[pl.ds(spot_of(at, 3), SHARD), :].astype(bf16)
    after_ref[:, E:] = half[:, :LEFT]
    before_ref[:, :E] = total_ref[pl.ds(spot_of(at, 5), SHARD), :].astype(bf16)
    before_ref[:, E:] = half[:, LEFT:]


def chunk_out(total_ref, at, targets, stage_ref, sems):
    copies = []
    slot = 0
    for n, d, cols in (
        (3, 3, None),
        (6, 5, None),
        (4, 4, pl.ds(0, LEFT)),
        (5, 4, pl.ds(LEFT, RIGHT)),
        (1, 1, None),
        (8, 7, None),
        (2, 2, None),
        (7, 6, None),
        (0, 0, None),
    ):
        rows = pl.ds(spot_of(at, d), SHARD)
        if d in (0, 2, 6):
            source = total_ref.at[rows, :]
        else:
            if n != 5:
                stage_ref[slot] = total_ref[rows, :].astype(bf16)
                slot += 1
            source = stage_ref.at[slot - 1] if cols is None else stage_ref.at[slot - 1, :, cols]
        copies.append(pltpu.make_async_copy(source, targets[n], sems.at[n]))
        copies[-1].start()
    return copies


def chunk_store(total_ref, at, targets):
    far_parts(total_ref, at, targets[3], targets[6])
    for n in (0, 1, 2, 4, 5):
        targets[n][...] = total_ref[pl.ds(spot_of(at, PLACES[n]), SHARD), :]


def align_body(at_ref, teacher_hbm, patch_ref, picks_ref, rows_hbm, send_hbm, teacher_ref, rows_ref, own_ref, extra_ref, sems):
    copy = pltpu.make_async_copy(teacher_hbm, teacher_ref, sems.at[GROUPS])
    copy.start()
    for j in range(GROUPS):
        extra_ref[j] = jnp.full(extra_ref.shape[1:], picks_ref[j], jnp.int32).astype(f32).astype(bf16)
    extra = pltpu.make_async_copy(extra_ref, send_hbm.at[:, :, pl.ds(E, E_WIDE - E)], sems.at[GROUPS + 1])
    extra.start()
    copy.wait()
    teacher = teacher_ref[...].astype(f32)
    unit = (teacher * lax.rsqrt(jnp.sum(teacher * teacher, axis=-1, keepdims=True) + eps)).astype(bf16)
    ids = lax.broadcasted_iota(jnp.int32, (teacher.shape[0], ROWS), 0)
    hot = (ids == patch_ref[...] - at_ref[1] * teacher.shape[0]).astype(f32).astype(bf16)
    rows_ref[...] = lax.dot_general(
        hot, unit, (((0,), (0,)), ((), ())), preferred_element_type=f32
    ).astype(bf16)
    copies = [pltpu.make_async_copy(rows_ref, rows_hbm, sems.at[GROUPS])]
    copies[0].start()
    own_ref[...] = rows_ref[pl.ds(spot_of(at_ref[0], 0), SHARD), :]
    for j in range(GROUPS):
        copies.append(pltpu.make_async_copy(own_ref, send_hbm.at[j, :, pl.ds(0, E)], sems.at[j]))
        copies[-1].start()
    copies.append(extra)
    for copy in copies:
        copy.wait()


def align(at, teacher, patch, picks):
    return pl.pallas_call(
        align_body,
        out_shape=[
            pltpu.HBM((ROWS, E), bf16),
            pltpu.HBM((GROUPS, SHARD, E_WIDE), bf16),
        ],
        in_specs=[IN_SMEM] + in_place(1) + in_vmem(1) + [IN_SMEM],
        out_specs=in_place(2),
        scratch_shapes=[
            pltpu.VMEM(teacher.shape, bf16),
            pltpu.VMEM((ROWS, E), bf16),
            pltpu.VMEM((SHARD, E), bf16),
            pltpu.VMEM((GROUPS, SHARD, E_WIDE - E), bf16),
            pltpu.SemaphoreType.DMA((GROUPS + 2,)),
        ],
        compiler_params=scoped(12),
        cost_estimate=pl.CostEstimate(flops=250_000_000, bytes_accessed=4_000_000, transcendentals=0),
        name="align",
    )(at, hbm(teacher), patch, picks)


def forward_body(at_ref, hidden_ref, w_in_ref, w_out_ref, pre_hbm, act_hbm, *refs):
    targets = refs[: NT + 1]
    total_ref, pre_ref, act_ref, sems, stage_ref, stage_sems = refs[NT + 1 :]
    pre = jnp.dot(hidden_ref[...], w_in_ref[...], preferred_element_type=f32)
    pre_ref[...] = pre
    act = (pre / (1.0 + jnp.exp(-pre))).astype(bf16)
    act_ref[...] = act
    copies = [
        pltpu.make_async_copy(pre_ref, pre_hbm, sems.at[0]),
        pltpu.make_async_copy(act_ref, act_hbm, sems.at[1]),
    ]
    for copy in copies:
        copy.start()
    total_ref[...] = jnp.dot(act, w_out_ref[...], preferred_element_type=f32)
    copies += chunk_out(total_ref, at_ref[0], targets, stage_ref, stage_sems)
    for copy in copies:
        copy.wait()


def forward(at, hidden_states, w_in, w_out):
    rows, width = hidden_states.shape[0], w_in.shape[1]
    return pl.pallas_call(
        forward_body,
        out_shape=[pltpu.HBM((rows, width), f32), pltpu.HBM((rows, width), bf16)] + SPLIT,
        in_specs=[IN_SMEM] + in_vmem(3),
        out_specs=in_place(3 + NT),
        scratch_shapes=[
            pltpu.VMEM((rows, E), f32),
            pltpu.VMEM((rows, width), f32),
            pltpu.VMEM((rows, width), bf16),
            pltpu.SemaphoreType.DMA((2,)),
        ]
        + STAGE,
        compiler_params=scoped(16),
        cost_estimate=pl.CostEstimate(flops=900_000_000, bytes_accessed=8_000_000, transcendentals=100_000),
        name="forward",
    )(at, hidden_states, w_in, w_out)


RECEIVED = 4


def normalise_body(local_ref, own_hbm, theirs_hbm, *refs):
    parts, refs = refs[: RECEIVED], refs[RECEIVED :]
    unit_hbm, inv_hbm, row_hbm, send_hbm, unit_ref, inv_ref, row_ref, got_ref, theirs_ref, sems = refs
    first = pltpu.make_async_copy(own_hbm, unit_ref, sems.at[RECEIVED + 1])
    first.start()
    copies = [pltpu.make_async_copy(parts[i], got_ref.at[i], sems.at[i]) for i in range(RECEIVED)]
    picks = pltpu.make_async_copy(
        theirs_hbm.at[:, pl.ds(0, 16), pl.ds(E, E_WIDE - E)], theirs_ref, sems.at[RECEIVED]
    )
    for copy in copies:
        copy.start()
    picks.start()
    first.wait()
    total = unit_ref[...]
    for i in range(RECEIVED):
        copies[i].wait()
        total = total + got_ref[i].astype(f32)
    inv = lax.rsqrt(jnp.sum(total * total, axis=-1, keepdims=True) + eps)
    unit = total * inv
    row_ref[:, :E] = unit.astype(bf16)
    copies = [
        pltpu.make_async_copy(row_ref.at[:, pl.ds(0, E)], send_hbm.at[j], sems.at[RECEIVED + 4 + j]) for j in range(GROUPS)
    ]
    for copy in copies:
        copy.start()
    unit_ref[...] = unit
    inv_ref[...] = jnp.broadcast_to(inv, inv_ref.shape)
    copies.append(pltpu.make_async_copy(unit_ref, unit_hbm, sems.at[RECEIVED + 1]))
    copies[-1].start()
    copies.append(pltpu.make_async_copy(inv_ref, inv_hbm, sems.at[RECEIVED + 2]))
    copies[-1].start()
    shape = (16, E_WIDE - E)
    lane = lax.broadcasted_iota(jnp.int32, shape, 1)
    block = lax.broadcasted_iota(jnp.int32, shape, 0)
    group, end = lane // RB, lane % RB
    picks.wait()
    other = jnp.zeros(shape, f32)
    for j in range(GROUPS):
        other = other + jnp.where(group == j, theirs_ref[j].astype(f32), 0.0)
    as_row = (local_ref[0:1, :] == block) & (local_ref[1:2, :] == end)
    as_key = (local_ref[2:3, :] == block) & (other.astype(jnp.int32) == end)
    counts = as_row.astype(f32) + as_key.astype(f32)
    counts = jnp.where((group < GROUPS) & (block < RB), counts, 0.0)
    row_ref[:, E:] = jnp.concatenate([counts, jnp.zeros((SHARD - 16, E_WIDE - E), f32)], axis=0).astype(bf16)
    copies.append(pltpu.make_async_copy(row_ref, row_hbm, sems.at[RECEIVED + 3]))
    copies[-1].start()
    for copy in copies:
        copy.wait()


def normalise(own, local, theirs, parts):
    return pl.pallas_call(
        normalise_body,
        out_shape=[
            pltpu.HBM((SHARD, E), f32),
            pltpu.HBM((SHARD, BLK), f32),
            pltpu.HBM((SHARD, E_WIDE), bf16),
            pltpu.HBM((GROUPS, SHARD, E), bf16),
        ],
        in_specs=in_vmem(1) + in_place(RECEIVED + 2),
        out_specs=in_place(4),
        scratch_shapes=[
            pltpu.VMEM((SHARD, E), f32),
            pltpu.VMEM((SHARD, BLK), f32),
            pltpu.VMEM((SHARD, E_WIDE), bf16),
            pltpu.VMEM((RECEIVED, SHARD, E), bf16),
            pltpu.VMEM((GROUPS, 16, E_WIDE - E), bf16),
            pltpu.SemaphoreType.DMA((RECEIVED + 4 + GROUPS,)),
        ],
        compiler_params=scoped(12),
        cost_estimate=pl.CostEstimate(flops=1_000_000, bytes_accessed=4_000_000, transcendentals=0),
        name="normalise",
    )(local, hbm(own), theirs, *[hbm(part) for part in parts])


def gather_in(at, pieces, target_ref, wide, sems):
    copies = []

    def bring(source, d, start, size):
        rows = pl.ds(spot_of(at, d), SHARD)
        copies.append(pltpu.make_async_copy(source, target_ref.at[rows, pl.ds(start, size)], sems.at[len(copies)]))
        copies[-1].start()

    for n in range(PARTS):
        source = pieces[n]
        if n in (3, 6):
            start, size = (LEFT, wide - LEFT) if n == 3 else (0, LEFT)
            bring(source.at[:, pl.ds(wide, size)], 4, start, size)
            source = source.at[:, pl.ds(0, wide)]
        bring(source, PLACES[n], 0, wide)
    return copies


def gram_body(at_ref, *refs):
    pieces, refs = dict(zip(PIECE_ORDER, refs[:PARTS])), refs[PARTS:]
    keys_hbm, teacher_hbm, spread_ref = refs[:3]
    refs = refs[3:]
    targets = refs[:PARTS]
    row_ref, key_ref, teacher_ref, grad_ref, total_ref, sems = refs[PARTS:]
    contract = (((1,), (1,)), ((), ()))
    step = 256
    spans = [pl.ds(k, step) for k in range(0, GROUPS * SHARD, step)]
    row_copies = gather_in(at_ref[0], pieces, row_ref, E_WIDE, sems)
    copies = []
    for i, span in enumerate(spans):
        pair = (
            pltpu.make_async_copy(keys_hbm.at[span, :], key_ref.at[span, :], sems.at[PARTS + 2 + 2 * i]),
            pltpu.make_async_copy(teacher_hbm.at[:, span], teacher_ref.at[:, span], sems.at[PARTS + 3 + 2 * i]),
        )
        pair[0].start()
        pair[1].start()
        copies.append(pair)
    for copy in row_copies:
        copy.wait()
    counts = jnp.zeros((16, E_WIDE - E), f32)
    for d in range(NT):
        counts = counts + row_ref[pl.ds(d * SHARD, 16), E:].astype(f32)
    tile = jnp.dot(counts.astype(bf16), spread_ref[...], preferred_element_type=f32) * (E / 8.0)
    for i, span in enumerate(spans):
        copies[i][0].wait()
        copies[i][1].wait()
        diff = (
            lax.dot_general(row_ref[:, :E], key_ref[span, :], contract, preferred_element_type=f32)
            - teacher_ref[:, span]
        )
        for a in range(RB):
            grad_ref[pl.ds(a * BLK, BLK), span] = (
                diff[a * BLK : (a + 1) * BLK] * tile[a : a + 1, i * step : (i + 1) * step]
            ).astype(bf16)
    for c, wide in ((0, 768), (768, 640)):
        total_ref[:, pl.ds(c, wide)] = jnp.dot(
            grad_ref[...], key_ref[:, pl.ds(c, wide)], preferred_element_type=f32
        )
    chunk_store(total_ref, at_ref[0], targets)


def gram_grads(at, pieces, keys, gram_teacher, spread):
    steps = GROUPS * SHARD // 256
    return pl.pallas_call(
        gram_body,
        out_shape=[jax.ShapeDtypeStruct(chunk.shape, chunk.dtype) for chunk in CHUNKS],
        in_specs=[IN_SMEM] + in_place(PARTS + 2) + in_vmem(1),
        out_specs=in_vmem(PARTS),
        scratch_shapes=[
            pltpu.VMEM((ROWS, E_WIDE), bf16),
            pltpu.VMEM((GROUPS * SHARD, E), bf16),
            pltpu.VMEM((ROWS, GROUPS * SHARD), f32),
            pltpu.VMEM((ROWS, GROUPS * SHARD), bf16),
            pltpu.VMEM((ROWS, E), f32),
            pltpu.SemaphoreType.DMA((PARTS + 2 + 2 * steps,)),
        ],
        compiler_params=scoped(20),
        cost_estimate=pl.CostEstimate(flops=1_700_000_000, bytes_accessed=9_000_000, transcendentals=0),
        name="gram_grads",
    )(at, *[hbm(pieces[n]) for n in PIECE_ORDER], keys, hbm(gram_teacher), spread)


def split_in(at, pieces, target_ref, wide, sems):
    copies = []
    for n in range(NT + 1):
        d = n if n <= 4 else n - 1
        cols = {4: pl.ds(0, LEFT), 5: pl.ds(LEFT, wide - LEFT)}.get(n, pl.ds(0, wide))
        rows = pl.ds(spot_of(at, d), SHARD)
        copies.append(pltpu.make_async_copy(pieces[n], target_ref.at[rows, cols], sems.at[n]))
        copies[-1].start()
    return copies


SPLIT_ORDER = (0, 1, 8, 2, 7, 3, 6, 4, 5)


def backward_body(at_ref, *refs):
    pieces, refs = dict(zip(SPLIT_ORDER, refs[: NT + 1])), refs[NT + 1 :]
    hidden_ref, w_out_ref, pre_ref, act_ref = refs[:4]
    keep_hbm, give_hbm, grad_pre_hbm, keep_ref, give_ref, grad_pre_ref, proj_ref, sems = refs[4:]
    at, tea = at_ref[0], at_ref[1]
    contract = (((1,), (1,)), ((), ()))
    over_rows = (((0,), (0,)), ((), ()))
    copies = split_in(at, pieces, proj_ref, E, sems)
    proj_ref[:, E:] = jnp.zeros((ROWS, E_PAD - E), bf16)
    pre = pre_ref[...]
    sigma = 1.0 / (1.0 + jnp.exp(-pre))
    slope = sigma * (1.0 + pre * (1.0 - sigma))
    for copy in copies:
        copy.wait()
    grad_act = lax.dot_general(proj_ref[:, :E], w_out_ref[...], contract, preferred_element_type=f32)
    grad_pre = (grad_act * slope).astype(bf16)
    grad_pre_ref[...] = grad_pre
    copies = [pltpu.make_async_copy(grad_pre_ref, grad_pre_hbm, sems.at[0])]
    copies[0].start()
    d_half, e_half = hidden_ref.shape[1] // 2, E_PAD // 2
    in_rows, out_rows = d_half // GROUPS, e_half // GROUPS
    for n, (ref, target, side) in enumerate(((keep_ref, keep_hbm, tea), (give_ref, give_hbm, 1 - tea))):
        part = hidden_ref[:, pl.ds(pl.multiple_of(side * d_half, d_half), d_half)]
        grad = lax.dot_general(part, grad_pre, over_rows, preferred_element_type=f32)
        for c in range(GROUPS):
            ref[c, pl.ds(0, in_rows), :] = grad[c * in_rows : (c + 1) * in_rows].astype(ref.dtype)
        part = proj_ref[:, pl.ds(pl.multiple_of(side * e_half, e_half), e_half)]
        grad = lax.dot_general(part, act_ref[...], over_rows, preferred_element_type=f32)
        for c in range(GROUPS):
            ref[c, pl.ds(in_rows, out_rows), :] = grad[c * out_rows : (c + 1) * out_rows].astype(ref.dtype)
        copies.append(pltpu.make_async_copy(ref, target, sems.at[n + 1]))
        copies[-1].start()
    for copy in copies:
        copy.wait()


def backward(where, pieces, hidden_states, w_out, pre_act, activation):
    rows, d_model = hidden_states.shape
    width = activation.shape[1]
    halves = (GROUPS, (d_model + E_PAD) // 2 // GROUPS, width)
    return pl.pallas_call(
        backward_body,
        out_shape=[
            pltpu.HBM(halves, bf16),
            pltpu.HBM(halves, bf16),
            pltpu.HBM((rows, width), bf16),
        ],
        in_specs=[IN_SMEM] + in_place(NT + 1) + in_vmem(4),
        out_specs=in_place(3),
        scratch_shapes=[
            pltpu.VMEM(halves, bf16),
            pltpu.VMEM(halves, bf16),
            pltpu.VMEM((rows, width), bf16),
            pltpu.VMEM((ROWS, E_PAD), bf16),
            pltpu.SemaphoreType.DMA((NT + 1,)),
        ],
        compiler_params=scoped(14),
        cost_estimate=pl.CostEstimate(flops=1_200_000_000, bytes_accessed=9_000_000, transcendentals=100_000),
        name="backward",
    )(where, *[pieces[d] for d in SPLIT_ORDER], hidden_states, w_out, pre_act, activation)


def hidden_body(grad_pre_hbm, w_in_ref, terms_hbm, grad_pre_ref, terms_ref, sems):
    first = pltpu.make_async_copy(grad_pre_hbm, grad_pre_ref, sems.at[NT])
    first.start()
    contract = (((1,), (1,)), ((), ()))
    share = w_in_ref.shape[0] // NT
    copies = []
    first.wait()
    for d in range(NT):
        span = pl.ds(d * ROWS, ROWS)
        terms_ref[span, :] = lax.dot_general(
            grad_pre_ref[...], w_in_ref[pl.ds(d * share, share), :], contract, preferred_element_type=f32
        ).astype(bf16)
        copies.append(pltpu.make_async_copy(terms_ref.at[span, :], terms_hbm.at[span, :], sems.at[d]))
        copies[-1].start()
    for copy in copies:
        copy.wait()


def hidden_grads(grad_pre, w_in):
    shape = (NT * ROWS, w_in.shape[0] // NT)
    return pl.pallas_call(
        hidden_body,
        out_shape=pltpu.HBM(shape, bf16),
        in_specs=in_place(1) + in_vmem(1),
        out_specs=in_place(1)[0],
        scratch_shapes=[
            pltpu.VMEM(grad_pre.shape, bf16),
            pltpu.VMEM(shape, bf16),
            pltpu.SemaphoreType.DMA((NT + 1,)),
        ],
        compiler_params=scoped(6),
        cost_estimate=pl.CostEstimate(flops=600_000_000, bytes_accessed=4_000_000, transcendentals=0),
        name="hidden_grads",
    )(hbm(grad_pre), w_in)


def pair_body(keep_ref, got_ref, sum_ref):
    sum_ref[...] = (keep_ref[...].astype(f32) + got_ref[...].astype(f32)).astype(bf16)


def pair_sum(keep, got):
    return pl.pallas_call(
        pair_body,
        out_shape=jax.ShapeDtypeStruct(keep.shape, bf16),
        in_specs=in_vmem(2),
        out_specs=in_vmem(1)[0],
        compiler_params=scoped(8),
        cost_estimate=pl.CostEstimate(flops=600_000, bytes_accessed=5_000_000, transcendentals=0),
        name="pair_sum",
    )(keep, got)


def half_out(ref, side, w_in_hbm, w_out_hbm, w_in_ref, w_out_ref, flat_ref, sems):
    d_half, e_half = w_in_ref.shape[0], E_PAD // 2
    in_rows, out_rows = d_half // GROUPS, e_half // GROUPS
    for c in range(GROUPS):
        w_in_ref[pl.ds(c * in_rows, in_rows), :] = ref[c, pl.ds(0, in_rows), :].astype(f32)
    copy = pltpu.make_async_copy(
        w_in_ref, w_in_hbm.at[pl.ds(pl.multiple_of(side * d_half, d_half), d_half), :], sems.at[0]
    )
    copy.start()
    for c in range(GROUPS):
        flat_ref[pl.ds(c * out_rows, out_rows), :] = ref[c, pl.ds(in_rows, out_rows), :].astype(f32)
    for c in range(0, e_half, BLK):
        w_out_ref[:, pl.ds(c, BLK)] = flat_ref[pl.ds(c, BLK), :].T
    for which, start, size in ((0, 0, e_half), (1, e_half, E - e_half)):

        @pl.when(side == which)
        def _():
            part = pltpu.make_async_copy(
                w_out_ref.at[:, pl.ds(0, size)], w_out_hbm.at[:, pl.ds(start, size)], sems.at[1]
            )
            part.start()
            part.wait()

    copy.wait()


def first_body(tea_ref, mine_ref, sum_hbm, w_in_hbm, w_out_hbm, hidden_ref, w_in_ref, w_out_ref, flat_ref, sum_ref, sems):
    copy = pltpu.make_async_copy(sum_hbm, sum_ref, sems.at[2])
    copy.start()
    half_out(mine_ref, tea_ref[0], w_in_hbm, w_out_hbm, w_in_ref, w_out_ref, flat_ref, sems)
    copy.wait()
    hidden_ref[...] = sum_ref[...].astype(f32)


def second_body(tea_ref, other_ref, w_in_old, w_out_old, w_in_hbm, w_out_hbm, w_in_ref, w_out_ref, flat_ref, sems):
    half_out(other_ref, 1 - tea_ref[0], w_in_hbm, w_out_hbm, w_in_ref, w_out_ref, flat_ref, sems)


def half_scratch(d_model, width):
    return [
        pltpu.VMEM((d_model // 2, width), f32),
        pltpu.VMEM((width, E_PAD // 2), f32),
        pltpu.VMEM((E_PAD // 2, width), f32),
    ]


def first_half(tea, mine, hidden, d_model):
    width = mine.shape[-1]
    return pl.pallas_call(
        first_body,
        out_shape=[
            pltpu.HBM((d_model, width), f32),
            pltpu.HBM((width, E), f32),
            jax.ShapeDtypeStruct(hidden.shape, f32),
        ],
        in_specs=[IN_SMEM] + in_vmem(1) + in_place(1),
        out_specs=in_place(2) + in_vmem(1),
        scratch_shapes=half_scratch(d_model, width)
        + [pltpu.VMEM(hidden.shape, bf16), pltpu.SemaphoreType.DMA((3,))],
        compiler_params=scoped(12),
        cost_estimate=pl.CostEstimate(flops=0, bytes_accessed=5_000_000, transcendentals=0),
        name="first_half",
    )(tea, mine, hbm(hidden))


def second_half(tea, other, w_in, w_out):
    return pl.pallas_call(
        second_body,
        out_shape=[pltpu.HBM(w_in.shape, f32), pltpu.HBM(w_out.shape, f32)],
        in_specs=[IN_SMEM] + in_vmem(1) + in_place(2),
        out_specs=in_place(2),
        scratch_shapes=half_scratch(w_in.shape[0], w_in.shape[1]) + [pltpu.SemaphoreType.DMA((2,))],
        input_output_aliases={2: 0, 3: 1},
        compiler_params=scoped(12),
        cost_estimate=pl.CostEstimate(flops=0, bytes_accessed=4_000_000, transcendentals=0),
        name="second_half",
    )(tea, other, hbm(w_in), hbm(w_out))


def on_device(hidden_states, w_in, w_out, teacher, patch_map, row_pick, key_pick):
    seq_index = lax.axis_index("seq")
    tp_index = lax.axis_index("tp")
    tea_index = lax.axis_index("tea")
    at = jnp.full((1,), tp_index, jnp.int32)
    tea = jnp.full((1,), tea_index, jnp.int32)
    contract = (((1,), (1,)), ((), ()))

    picks = row_pick.reshape(GROUPS)
    group = jnp.full((1,), lax.axis_index(("seq", "tea")), jnp.int32)
    row_teacher, teacher_send = align(jnp.concatenate([at, group]), teacher, patch_map.reshape(1, ROWS), picks)
    teacher_send, at_next = lax.optimization_barrier((teacher_send, at))
    teacher_got = lax.all_to_all(teacher_send, "seq", 0, 0, tiled=True)

    pre_act, activation, *chunks = forward(at_next, hidden_states, w_in, w_out)
    activation, key_pick, picks = lax.optimization_barrier((activation, key_pick, picks))
    received = sum_split(*chunks)

    table = key_pick.reshape(GROUPS, GROUPS)
    of_rows = lax.dynamic_index_in_dim(table, seq_index, axis=0, keepdims=False)
    of_keys = lax.dynamic_index_in_dim(table, seq_index, axis=1, keepdims=False)
    local = jnp.repeat(jnp.stack([picks, of_rows, of_keys]), RB, axis=1)
    local = jnp.pad(local, ((0, 8 - 3), (0, E_WIDE - E - GROUPS * RB)))
    key_ids = jnp.arange(GROUPS * SHARD, dtype=jnp.int32)
    key_cell = key_ids // SHARD * RB + (tp_index * SHARD + key_ids % SHARD) // BLK
    spread = (jnp.arange(E_WIDE - E, dtype=jnp.int32)[:, None] == key_cell[None, :]).astype(bf16)

    *received, teacher_got = lax.optimization_barrier((*received, teacher_got))
    unit_student, inv_norm, row_send, key_send = normalise(chunks[0], local, teacher_got, received)
    rows = gather_ring(row_send)
    keys = lax.all_to_all(key_send, "seq", 0, 0, tiled=True).reshape(GROUPS * SHARD, E)
    teacher_got, inv_norm = lax.optimization_barrier((teacher_got, inv_norm))
    inv_norm = inv_norm[:, :1]
    key_teacher = teacher_got[:, :, :E].reshape(GROUPS * SHARD, E)
    gram_teacher = lax.dot_general(row_teacher, key_teacher, contract, preferred_element_type=f32)

    row_grad = gram_grads(at, rows, keys, gram_teacher, spread)
    unit_grad = row_grad[0]
    for piece in sum_ring(*row_grad):
        unit_grad = unit_grad + piece.astype(f32)
    inner = jnp.sum(unit_student * unit_grad, axis=-1, keepdims=True)
    grad_proj = ((unit_grad - unit_student * inner) * inv_norm).astype(bf16)
    pieces = gather_split(grad_proj)

    where = jnp.concatenate([at, tea])
    keep, give, grad_pre = backward(where, pieces, hidden_states, w_out, pre_act, activation)
    got = swap_tea(give)
    hidden_terms = hidden_grads(grad_pre, w_in)
    chip, hidden_terms = lax.optimization_barrier((pair_sum(keep, got), hidden_terms))
    hidden_sum = lax.psum_scatter(hidden_terms, "tp", scatter_dimension=0, tiled=True)
    chip = lax.all_to_all(chip, "seq", 0, 0, tiled=True)
    mine = to_all(jnp.sum(chip.astype(f32), axis=0).astype(bf16)).reshape(keep.shape)
    other = swap_tea(mine)
    grad_w_in, grad_w_out, grad_hidden = first_half(tea, mine, hidden_sum, hidden_states.shape[1])
    grad_w_in, grad_w_out = second_half(tea, other, grad_w_in, grad_w_out)
    return (grad_hidden, grad_w_in, grad_w_out)


def solution(mesh):
    return jax.shard_map(
        on_device,
        mesh=mesh,
        in_specs=(
            P(("seq", "tea"), None),
            P(None, "tp"),
            P("tp", None),
            P(("seq", "tea"), None),
            P(("seq", "tea")),
            P("seq", "tp", "tea", None),
            P(None, "tp", "tea", None),
        ),
        out_specs=(P(("seq", "tea"), "tp"), P(None, "tp"), P("tp", None)),
        check_vma=False,
    )
```

profile of v0, /device:TPU:1, one launch (start us, length us, event | category | flops | bytes accessed | tf_op | source)
XLA Modules:
  0.0 215.5 jit_solution(4122121037943835247)
XLA Ops:
  7.2 0.7 reshape.63.patch_ref
  7.9 0.7 copy-done.9
  8.6 4.1 %align.1 = (bf16[384,1408]{1,0:T(8,128)(2,1)}, bf16[16,48,1536]{2,1,0:T(8,128)(2,1)}) custom-call(s32[2]{0:T(128)S(1)} %pad_add_fusion.2.at_ref, bf16[192,1408]{1,0:T(8,128)(2,1)} %teacher_hbm.1, s32[1,384]{1,0:T(1,128)S(1)} %reshape.63.patch_ref, s32[16]{0:T(128)S(1)} %bitcast.12), custom_call_target="tpu_custom_call" | custom-call | flops 250000000 | bytes 4000000 | tf_op jit(solution)/shard_map/align/pallas_call | solution.py:188
  12.8 7.7 %all-to-all-start = ((bf16[16,48,1536]{2,1,0:T(8,128)(2,1)}), bf16[16,48,1536]{2,1,0:T(8,128)(2,1)S(1)}, u32[]{:S(2)}, u32[]{:S(2)}) async-start(bf16[16,48,1536]{2,1,0:T(8,128)(2,1)} %get-tuple-element.63), calls=%async_computation | async-start | bytes 4718592 | tf_op jit(solution)/shard_map/all_to_all | solution.py:627
  20.5 1.7 copy-done.1
  22.2 1.4 copy-done.3
  23.6 2.9 %forward.1 = (f32[384,256]{1,0:T(8,128)}, bf16[384,256]{1,0:T(8,128)(2,1)}, f32[48,1408]{1,0:T(8,128)}, bf16[48,1408]{1,0:T(8,128)(2,1)}, f32[48,1408]{1,0:T(8,1...) custom-call(s32[1]{0:T(128)} %bitcast.1.at_ref, ...), custom_call_target="tpu_custom_call" | custom-call | flops 900000000 | bytes 8000000 | tf_op jit(solution)/shard_map/forward/pallas_call | solution.py:230
  26.5 1.7 collective-permute-start.2
  28.2 3.0 %collective-permute-start.3 = (bf16[48,768]{1,0:T(8,128)(2,1)}, bf16[48,768]{1,0:T(8,128)(2,1)}, u32[]{:S(2)}, u32[]{:S(2)}) collective-permute-start(bf16[48,768]{1,0:T(8,128)(2,1)} %get-tuple-element.59), channel_id=1, source_target_pairs={{0,4},{2,6},{4,8},{6,10},{8,12},{10,14},{12,0},{14,2},{1,5},{3,7},... | collective-permute-start | bytes 221192 | tf_op jit(solution)/shard_map/ppermute | solution.py:25
  31.2 2.1 collective-permute-start.6
  33.4 0.7 collective-permute-start
  34.1 2.0 collective-permute-start.1
  36.0 2.3 %collective-permute-done.3 = bf16[48,768]{1,0:T(8,128)(2,1)} collective-permute-done((bf16[48,768]{1,0:T(8,128)(2,1)}, bf16[48,768]{1,0:T(8,128)(2,1)}, u32[]{:S(2)}, u32[]{:S(2)}) %collective-permute-start.3) | collective-permute-done | bytes 73760 | tf_op jit(solution)/shard_map/ppermute | solution.py:25
  38.3 1.0 collective-permute-start.5
  39.3 1.7 add_convert_fusion.3
  41.0 0.4 collective-permute-start.4
  41.4 1.3 collective-permute-done.5
  42.7 1.7 add_convert_fusion.2
  44.4 2.0 collective-permute-start.7
  46.4 0.4 dynamic-slice_reduce_fusion
  47.1 0.3 collective-permute-done.4.refs_2_
  47.4 5.1 %collective-permute-done.7.refs_3_ = bf16[48,1408]{1,0:T(8,128)(2,1)} collective-permute-done((bf16[48,1408]{1,0:T(8,128)(2,1)}, bf16[48,1408]{1,0:T(8,128)(2,1)}, u32[]{:S(2)}, u32[]{:S(2)}) %collective-permute-start.7) | collective-permute-done | bytes 135200 | tf_op jit(solution)/shard_map/ppermute | solution.py:25
  52.5 2.6 %all-to-all-done.theirs_hbm = bf16[16,48,1536]{2,1,0:T(8,128)(2,1)S(1)} async-done(((bf16[16,48,1536]{2,1,0:T(8,128)(2,1)}), bf16[16,48,1536]{2,1,0:T(8,128)(2,1)S(1)}, u32[]{:S(2)}, u32[]{:S(2)}) %all-to-all-start) | async-done | bytes 2359328 | tf_op jit(solution)/shard_map/all_to_all | solution.py:627
  55.1 3.0 %normalise.1 = (f32[48,1408]{1,0:T(8,128)}, f32[48,128]{1,0:T(8,128)}, bf16[48,1536]{1,0:T(8,128)(2,1)}, bf16[16,48,1408]{2,1,0:T(8,128)(2,1)}) custom-call(s32[8,128]{1,0:T(8,128)S(1)} %pad.10.local_ref, f32[48,1408]{1,0:T(8,128)} %get-tuple-element.54.own_hbm, bf16[16,48,1536]{2,1,0:T(8,128)(2,1)S(1)} %all-to-all-done.theirs_hbm, ...), custom_call_target="tpu_custom_call" | custom-call | flops 1000000 | bytes 4000000 | tf_op jit(solution)/shard_map/normalise/pallas_call | solution.py:302
  58.1 4.4 %all-to-all-start.1 = ((bf16[16,48,1408]{2,1,0:T(8,128)(2,1)}), bf16[16,48,1408]{2,1,0:T(8,128)(2,1)}, u32[]{:S(2)}, u32[]{:S(2)}) async-start(bf16[16,48,1408]{2,1,0:T(8,128)(2,1)} %get-tuple-element.70), calls=%async_computation.1 | async-start | bytes 4325376 | tf_op jit(solution)/shard_map/all_to_all | solution.py:645
  62.6 6.1 %collective-permute-start.10 = (bf16[48,1536]{1,0:T(8,128)(2,1)}, bf16[48,1536]{1,0:T(8,128)(2,1)S(1)}, u32[]{:S(2)}, u32[]{:S(2)}) collective-permute-start(bf16[48,1536]{1,0:T(8,128)(2,1)} %get-tuple-element.69.refs_0_), channel_id=1, source_target_pairs={{0,12},{2,14},{4,0},{6,2},{8,4},{10,6},{12,8},{14,10},{1,13},{3,15... | collective-permute-start | bytes 442376 | tf_op jit(solution)/shard_map/ppermute | solution.py:25
  68.7 0.7 collective-permute-start.8
  69.5 1.3 collective-permute-start.11
  70.9 0.6 collective-permute-done.10.refs_3_
  71.6 6.3 %collective-permute-done.8.refs_1_ = bf16[48,1536]{1,0:T(8,128)(2,1)S(1)} collective-permute-done((bf16[48,1536]{1,0:T(8,128)(2,1)}, bf16[48,1536]{1,0:T(8,128)(2,1)S(1)}, u32[]{:S(2)}, u32[]{:S(2)}) %collective-permute-start.8) | collective-permute-done | bytes 147488 | tf_op jit(solution)/shard_map/ppermute | solution.py:25
  77.9 1.6 collective-permute-start.12
  79.6 2.1 collective-permute-done.9.refs_2_
  81.8 2.1 fusion.18.refs_8_
  83.9 0.9 collective-permute-done.12.refs_5_
  84.8 9.0 %collective-permute-done.13.refs_6_ = bf16[48,2304]{1,0:T(8,128)(2,1)S(1)} collective-permute-done((bf16[48,2304]{1,0:T(8,128)(2,1)S(1)}, bf16[48,2304]{1,0:T(8,128)(2,1)S(1)}, u32[]{:S(2)}, u32[]{:S(2)}) %collective-permute-start.13) | collective-permute-done | bytes 221216 | tf_op jit(solution)/shard_map/ppermute | solution.py:25
  93.8 0.7 copy-done.21
  94.5 5.4 %gram_grads.1 = (f32[48,1408]{1,0:T(8,128)S(1)}, f32[48,1408]{1,0:T(8,128)S(1)}, f32[48,1408]{1,0:T(8,128)S(1)}, bf16[48,2176]{1,0:T(8,128)(2,1)S(1)}, f32[48,14...) custom-call(s32[1]{0:T(128)} %bitcast.1.at_ref, bf16[48,1536]{1,0:T(8,128)(2,1)} %get-tuple-element.69.refs_0_, ...), custom_call_target="tpu_custom_call" | custom-call | flops 1700000000 | bytes 9000000 | tf_op jit(solution)/shard_map/gram_grads/pallas_call | solution.py:389
  99.9 2.9 %collective-permute-start.16 = (bf16[48,2048]{1,0:T(8,128)(2,1)S(1)}, bf16[48,2048]{1,0:T(8,128)(2,1)S(1)}, u32[]{:S(2)}, u32[]{:S(2)}) collective-permute-start(bf16[48,2048]{1,0:T(8,128)(2,1)S(1)} %get-tuple-element.78), channel_id=1, source_target_pairs={{0,12},{2,14},{4,0},{6,2},{8,4},{10,6},{12,8},{14,10},{1,13},{3,15... | collective-permute-start | bytes 589832 | tf_op jit(solution)/shard_map/ppermute | solution.py:25
  102.8 3.4 %collective-permute-done.16 = bf16[48,2048]{1,0:T(8,128)(2,1)S(1)} collective-permute-done((bf16[48,2048]{1,0:T(8,128)(2,1)S(1)}, bf16[48,2048]{1,0:T(8,128)(2,1)S(1)}, u32[]{:S(2)}, u32[]{:S(2)}) %collective-permute-start.16) | collective-permute-done | bytes 196640 | tf_op jit(solution)/shard_map/ppermute | solution.py:25
  106.3 3.4 %collective-permute-start.17 = (bf16[48,1408]{1,0:T(8,128)(2,1)S(1)}, bf16[48,1408]{1,0:T(8,128)(2,1)S(1)}, u32[]{:S(2)}, u32[]{:S(2)}) collective-permute-start(bf16[48,1408]{1,0:T(8,128)(2,1)S(1)} %add_convert_fusion), channel_id=1, source_target_pairs={{0,12},{2,14},{4,0},{6,2},{8,4},{10,6},{12,8},{14,10},{1,13},{3,15... | collective-permute-start | bytes 405512 | tf_op jit(solution)/shard_map/ppermute | solution.py:25
  109.7 4.8 %collective-permute-start.19 = (bf16[48,1408]{1,0:T(8,128)(2,1)S(1)}, bf16[48,1408]{1,0:T(8,128)(2,1)S(1)}, u32[]{:S(2)}, u32[]{:S(2)}) collective-permute-start(bf16[48,1408]{1,0:T(8,128)(2,1)S(1)} %fusion.1), channel_id=1, source_target_pairs={{0,14},{2,0},{4,2},{6,4},{8,6},{10,8},{12,10},{14,12},{1,15},{3,1}... | collective-permute-start | bytes 405512 | tf_op jit(solution)/shard_map/ppermute | solution.py:25
  114.6 2.4 %collective-permute-start.15 = (bf16[48,1408]{1,0:T(8,128)(2,1)S(1)}, bf16[48,1408]{1,0:T(8,128)(2,1)S(1)}, u32[]{:S(2)}, u32[]{:S(2)}) collective-permute-start(bf16[48,1408]{1,0:T(8,128)(2,1)S(1)} %add_convert_fusion.1), channel_id=1, source_target_pairs={{0,4},{2,6},{4,8},{6,10},{8,12},{10,14},{12,0},{14,2},{1,5},{3,7},... | collective-permute-start | bytes 405512 | tf_op jit(solution)/shard_map/ppermute | solution.py:25
  117.4 2.7 %collective-permute-done.19 = bf16[48,1408]{1,0:T(8,128)(2,1)S(1)} collective-permute-done((bf16[48,1408]{1,0:T(8,128)(2,1)S(1)}, bf16[48,1408]{1,0:T(8,128)(2,1)S(1)}, u32[]{:S(2)}, u32[]{:S(2)}) %collective-permute-start.19) | collective-permute-done | bytes 135200 | tf_op jit(solution)/shard_map/ppermute | solution.py:25
  120.1 0.9 collective-permute-done.15
  121.0 2.6 %collective-permute-done.18 = bf16[48,1408]{1,0:T(8,128)(2,1)S(1)} collective-permute-done((bf16[48,1408]{1,0:T(8,128)(2,1)S(1)}, bf16[48,1408]{1,0:T(8,128)(2,1)S(1)}, u32[]{:S(2)}, u32[]{:S(2)}) %collective-permute-start.18) | collective-permute-done | bytes 135200 | tf_op jit(solution)/shard_map/ppermute | solution.py:25
  124.0 3.6 %collective-permute-start.22 = (bf16[48,1408]{1,0:T(8,128)(2,1)S(1)}, bf16[48,1408]{1,0:T(8,128)(2,1)S(1)}, u32[]{:S(2)}, u32[]{:S(2)}) collective-permute-start(bf16[48,1408]{1,0:T(8,128)(2,1)S(1)} %multiply_convert_fusion.refs_0_), channel_id=1, source_target_pairs={{0,12},{2,14},{4,0},{6,2},{8,4},{10,6},{12,8},{14,10},{1,13},{3,15... | collective-permute-start | bytes 405512 | tf_op jit(solution)/shard_map/ppermute | solution.py:25
  127.6 0.6 collective-permute-start.21
  128.2 2.1 collective-permute-start.20
  130.3 0.8 collective-permute-done.23.refs_4_
  131.1 2.2 %collective-permute-start.25 = (bf16[48,1408]{1,0:T(8,128)(2,1)S(1)}, bf16[48,1408]{1,0:T(8,128)(2,1)S(1)}, u32[]{:S(2)}, u32[]{:S(2)}) collective-permute-start(bf16[48,1408]{1,0:T(8,128)(2,1)S(1)} %collective-permute-done.23.refs_4_), channel_id=1, source_target_pairs={{0,2},{2,4},{4,6},{6,8},{8,10},{10,12},{12,14},{14,0},{1,3},{3,5},... | collective-permute-start | bytes 405512 | tf_op jit(solution)/shard_map/ppermute | solution.py:25
  133.3 0.7 collective-permute-start.24
  134.0 0.4 collective-permute-start.26
  134.5 3.2 %collective-permute-start.27 = (bf16[48,640]{1,0:T(8,128)(2,1)S(1)}, bf16[48,640]{1,0:T(8,128)(2,1)S(1)}, u32[]{:S(2)}, u32[]{:S(2)}) collective-permute-start(bf16[48,640]{1,0:T(8,128)(2,1)S(1)} %slice.47), channel_id=1, source_target_pairs={{0,12},{2,14},{4,0},{6,2},{8,4},{10,6},{12,8},{14,10},{1,13},{3,15... | collective-permute-start | bytes 184328 | tf_op jit(solution)/shard_map/ppermute | solution.py:25
  137.8 2.4 %collective-permute-done.27.refs_8_ = bf16[48,640]{1,0:T(8,128)(2,1)S(1)} collective-permute-done((bf16[48,640]{1,0:T(8,128)(2,1)S(1)}, bf16[48,640]{1,0:T(8,128)(2,1)S(1)}, u32[]{:S(2)}, u32[]{:S(2)}) %collective-permute-start.27) | collective-permute-done | bytes 61472 | tf_op jit(solution)/shard_map/ppermute | solution.py:25
  140.2 0.9 collective-permute-done.26.refs_7_
  141.1 4.7 %backward.1 = (bf16[16,144,256]{2,1,0:T(8,128)(2,1)}, bf16[16,144,256]{2,1,0:T(8,128)(2,1)}, bf16[384,256]{1,0:T(8,128)(2,1)}) custom-call(s32[2]{0:T(128)S(1)} %pad_add_fusion.1.at_ref, bf16[48,1408]{1,0:T(8,128)(2,1)S(1)} %multiply_convert_fusion.refs_0_, bf16[48,1408]{1,0:T(8,128)(2,1)S(1)} %collective-permute-done.20.refs_1_, ...), custom_call_target="tpu_custom_call" | custom-call | flops 1200000000 | bytes 9000000 | tf_op jit(solution)/shard_map/backward/pallas_call | solution.py:462
  145.8 10.5 %collective-permute-start.28 = (bf16[16,144,256]{2,1,0:T(8,128)(2,1)}, bf16[16,144,256]{2,1,0:T(8,128)(2,1)S(1)}, u32[]{:S(2)}, u32[]{:S(2)}) collective-permute-start(bf16[16,144,256]{2,1,0:T(8,128)(2,1)} %get-tuple-element.86), channel_id=1, source_target_pairs={{0,1},{1,0},{2,3},{3,2},{4,5},{5,4},{6,7},{7,6},{8,9},{9,8},{10,11... | collective-permute-start | bytes 3538952 | tf_op jit(solution)/shard_map/ppermute | solution.py:29
  156.4 2.8 %hidden_grads.1 = bf16[3072,384]{1,0:T(8,128)(2,1)} custom-call(bf16[384,256]{1,0:T(8,128)(2,1)} %get-tuple-element.87.grad_pre_hbm, bf16[3072,256]{1,0:T(8,128)(2,1)S(1)} %copy-done.4), custom_call_target="tpu_custom_call" | custom-call | flops 600000000 | bytes 4000000 | tf_op jit(solution)/shard_map/hidden_grads/pallas_call | solution.py:504
  159.2 0.3 pair_sum.1
  159.5 22.0 %all_to_all.20 = bf16[16,144,256]{2,1,0:T(8,128)(2,1)S(1)} all-to-all(bf16[16,144,256]{2,1,0:T(8,128)(2,1)S(1)} %pair_sum.1), channel_id=1, replica_groups=mesh['seq'=16,'tp'=8,'tea'=2] {'seq'}, dimensions={0} | all-to-all | bytes 2359296 | tf_op jit(solution)/shard_map/all_to_all | solution.py:665
  181.8 20.3 %all_to_all.21.mine_ref = bf16[16,144,256]{2,1,0:T(8,128)(2,1)S(1)} all-to-all(bf16[16,144,256]{2,1,0:T(8,128)(2,1)S(1)} %broadcast_in_dim.25), channel_id=1, replica_groups=mesh['seq'=16,'tp'=8,'tea'=2] {'seq'}, dimensions={0} | all-to-all | bytes 2359296 | tf_op jit(solution)/shard_map/all_to_all | solution.py:77
  202.1 2.4 %collective-permute-start.29 = (bf16[16,144,256]{2,1,0:T(8,128)(2,1)S(1)}, bf16[16,144,256]{2,1,0:T(8,128)(2,1)S(1)}, u32[]{:S(2)}, u32[]{:S(2)}) collective-permute-start(bf16[16,144,256]{2,1,0:T(8,128)(2,1)S(1)} %all_to_all.21.mine_ref), channel_id=1, source_target_pairs={{0,1},{1,0},{2,3},{3,2},{4,5},{5,4},{6,7},{7,6},{8,9},{9,8},{10,11... | collective-permute-start | bytes 3538952 | tf_op jit(solution)/shard_map/ppermute | solution.py:29
  204.5 2.5 %first_half.1 = (f32[3072,256]{1,0:T(8,128)}, f32[256,1408]{1,0:T(8,128)}, f32[384,384]{1,0:T(8,128)}) custom-call(s32[1]{0:T(128)} %bitcast.tea_ref, bf16[16,144,256]{2,1,0:T(8,128)(2,1)S(1)} %all_to_all.21.mine_ref, bf16[384,384]{1,0:T(8,128)(2,1)} %reduce-scatter.2.cloned.1.call-done.sum_hbm), custom_call_target="tpu_custom_call" | custom-call | bytes 5000000 | tf_op jit(solution)/shard_map/first_half/pallas_call | solution.py:584
  207.0 1.7 second_half.1
  (94 shorter events, 2.0 us)
Async XLA Ops:
  7.2 39.2 %copy-start = (s32[16,1,1,16]{3,2,1,0:T(1,128)S(1)}, s32[16,1,1,16]{3,2,1,0:T(1,128)}, u32[]{:S(2)}) copy-start(s32[16,1,1,16]{3,2,1,0:T(1,128)} %param.13) | copy-start | bytes 3076
  7.9 0.7 copy-start.9
  12.7 7.8 %copy-start.5 = (bf16[256,1408]{1,0:T(8,128)(2,1)S(1)}, bf16[256,1408]{1,0:T(8,128)(2,1)}, u32[]{:S(2)}) copy-start(bf16[256,1408]{1,0:T(8,128)(2,1)} %refs_10_.1) | copy-start | bytes 2162692
  12.8 42.4 %all-to-all-start = ((bf16[16,48,1536]{2,1,0:T(8,128)(2,1)}), bf16[16,48,1536]{2,1,0:T(8,128)(2,1)S(1)}, u32[]{:S(2)}, u32[]{:S(2)}) async-start(bf16[16,48,1536]{2,1,0:T(8,128)(2,1)} %get-tuple-element.63), calls=%async_computation | async-start | bytes 4718592 | tf_op jit(solution)/shard_map/all_to_all | solution.py:627
  20.5 1.7 copy-start.1
  22.2 1.4 copy-start.3
  23.6 23.2 %copy-start.10 = (s32[1,1,1,16]{3,2,1,0:T(1,128)S(1)}, s32[1,1,1,16]{3,2,1,0:T(1,128)}, u32[]{:S(2)}) copy-start(s32[1,1,1,16]{3,2,1,0:T(1,128)} %param.12) | copy-start | bytes 196
  26.5 12.8 %collective-permute-start.2 = (bf16[48,1408]{1,0:T(8,128)(2,1)}, bf16[48,1408]{1,0:T(8,128)(2,1)S(1)}, u32[]{:S(2)}, u32[]{:S(2)}) collective-permute-start(bf16[48,1408]{1,0:T(8,128)(2,1)} %get-tuple-element.58), channel_id=1, source_target_pairs={{0,2},{2,4},{4,6},{6,8},{8,10},{10,12},{12,14},{14,0},{1,3},{3,5},... | collective-permute-start | bytes 405512 | tf_op jit(solution)/shard_map/ppermute | solution.py:25
  28.2 10.1 %collective-permute-start.3 = (bf16[48,768]{1,0:T(8,128)(2,1)}, bf16[48,768]{1,0:T(8,128)(2,1)}, u32[]{:S(2)}, u32[]{:S(2)}) collective-permute-start(bf16[48,768]{1,0:T(8,128)(2,1)} %get-tuple-element.59), channel_id=1, source_target_pairs={{0,4},{2,6},{4,8},{6,10},{8,12},{10,14},{12,0},{14,2},{1,5},{3,7},... | collective-permute-start | bytes 221192 | tf_op jit(solution)/shard_map/ppermute | solution.py:25
  31.2 10.2 %collective-permute-start.6 = (bf16[48,640]{1,0:T(8,128)(2,1)}, bf16[48,640]{1,0:T(8,128)(2,1)}, u32[]{:S(2)}, u32[]{:S(2)}) collective-permute-start(bf16[48,640]{1,0:T(8,128)(2,1)} %get-tuple-element.62), channel_id=1, source_target_pairs={{0,12},{2,14},{4,0},{6,2},{8,4},{10,6},{12,8},{14,10},{1,13},{3,15... | collective-permute-start | bytes 184328 | tf_op jit(solution)/shard_map/ppermute | solution.py:25
  33.4 13.7 %collective-permute-start = (bf16[48,1408]{1,0:T(8,128)(2,1)}, bf16[48,1408]{1,0:T(8,128)(2,1)S(1)}, u32[]{:S(2)}, u32[]{:S(2)}) collective-permute-start(bf16[48,1408]{1,0:T(8,128)(2,1)} %get-tuple-element.55), channel_id=1, source_target_pairs={{0,2},{2,4},{4,6},{6,8},{8,10},{10,12},{12,14},{14,0},{1,3},{3,5},... | collective-permute-start | bytes 405512 | tf_op jit(solution)/shard_map/ppermute | solution.py:25
  34.1 13.0 %collective-permute-start.1 = (bf16[48,1408]{1,0:T(8,128)(2,1)}, bf16[48,1408]{1,0:T(8,128)(2,1)S(1)}, u32[]{:S(2)}, u32[]{:S(2)}) collective-permute-start(bf16[48,1408]{1,0:T(8,128)(2,1)} %get-tuple-element.56), channel_id=1, source_target_pairs={{0,14},{2,0},{4,2},{6,4},{8,6},{10,8},{12,10},{14,12},{1,15},{3,1}... | collective-permute-start | bytes 405512 | tf_op jit(solution)/shard_map/ppermute | solution.py:25
  38.3 4.4 %collective-permute-start.5 = (bf16[48,1408]{1,0:T(8,128)(2,1)}, bf16[48,1408]{1,0:T(8,128)(2,1)S(1)}, u32[]{:S(2)}, u32[]{:S(2)}) collective-permute-start(bf16[48,1408]{1,0:T(8,128)(2,1)} %get-tuple-element.61), channel_id=1, source_target_pairs={{0,14},{2,0},{4,2},{6,4},{8,6},{10,8},{12,10},{14,12},{1,15},{3,1}... | collective-permute-start | bytes 405512 | tf_op jit(solution)/shard_map/ppermute | solution.py:25
  41.0 6.4 %collective-permute-start.4 = (bf16[48,1408]{1,0:T(8,128)(2,1)}, bf16[48,1408]{1,0:T(8,128)(2,1)S(1)}, u32[]{:S(2)}, u32[]{:S(2)}) collective-permute-start(bf16[48,1408]{1,0:T(8,128)(2,1)} %add_convert_fusion.3), channel_id=1, source_target_pairs={{0,4},{2,6},{4,8},{6,10},{8,12},{10,14},{12,0},{14,2},{1,5},{3,7},... | collective-permute-start | bytes 405512 | tf_op jit(solution)/shard_map/ppermute | solution.py:25
  44.4 8.1 %collective-permute-start.7 = (bf16[48,1408]{1,0:T(8,128)(2,1)}, bf16[48,1408]{1,0:T(8,128)(2,1)}, u32[]{:S(2)}, u32[]{:S(2)}) collective-permute-start(bf16[48,1408]{1,0:T(8,128)(2,1)} %add_convert_fusion.2), channel_id=1, source_target_pairs={{0,12},{2,14},{4,0},{6,2},{8,4},{10,6},{12,8},{14,10},{1,13},{3,15... | collective-permute-start | bytes 405512 | tf_op jit(solution)/shard_map/ppermute | solution.py:25
  47.0 8.1 %copy-start.14 = (bf16[48,1408]{1,0:T(8,128)(2,1)}, bf16[48,1408]{1,0:T(8,128)(2,1)S(1)}, u32[]{:S(2)}) copy-start(bf16[48,1408]{1,0:T(8,128)(2,1)S(1)} %collective-permute-done.refs_0_) | copy-start | bytes 405508
  47.1 8.1 %copy-start.15 = (bf16[48,1408]{1,0:T(8,128)(2,1)}, bf16[48,1408]{1,0:T(8,128)(2,1)S(1)}, u32[]{:S(2)}) copy-start(bf16[48,1408]{1,0:T(8,128)(2,1)S(1)} %collective-permute-done.1.refs_1_) | copy-start | bytes 405508
  47.4 7.7 %copy-start.16 = (bf16[48,1408]{1,0:T(8,128)(2,1)}, bf16[48,1408]{1,0:T(8,128)(2,1)S(1)}, u32[]{:S(2)}) copy-start(bf16[48,1408]{1,0:T(8,128)(2,1)S(1)} %collective-permute-done.4.refs_2_) | copy-start | bytes 405508
  58.1 35.7 %all-to-all-start.1 = ((bf16[16,48,1408]{2,1,0:T(8,128)(2,1)}), bf16[16,48,1408]{2,1,0:T(8,128)(2,1)}, u32[]{:S(2)}, u32[]{:S(2)}) async-start(bf16[16,48,1408]{2,1,0:T(8,128)(2,1)} %get-tuple-element.70), calls=%async_computation.1 | async-start | bytes 4325376 | tf_op jit(solution)/shard_map/all_to_all | solution.py:645
  62.6 141.9 %reduce-scatter.2.cloned.1.call-start = ((), (), s32[]{:S(2)}) async-start(), calls=%async_computation.5 | async-start | bytes 2654208 | tf_op jit(solution)/shard_map/reduce_scatter | solution.py:664
  62.6 8.9 %collective-permute-start.10 = (bf16[48,1536]{1,0:T(8,128)(2,1)}, bf16[48,1536]{1,0:T(8,128)(2,1)S(1)}, u32[]{:S(2)}, u32[]{:S(2)}) collective-permute-start(bf16[48,1536]{1,0:T(8,128)(2,1)} %get-tuple-element.69.refs_0_), channel_id=1, source_target_pairs={{0,12},{2,14},{4,0},{6,2},{8,4},{10,6},{12,8},{14,10},{1,13},{3,15... | collective-permute-start | bytes 442376 | tf_op jit(solution)/shard_map/ppermute | solution.py:25
  68.7 9.2 %collective-permute-start.8 = (bf16[48,1536]{1,0:T(8,128)(2,1)}, bf16[48,1536]{1,0:T(8,128)(2,1)S(1)}, u32[]{:S(2)}, u32[]{:S(2)}) collective-permute-start(bf16[48,1536]{1,0:T(8,128)(2,1)} %get-tuple-element.69.refs_0_), channel_id=1, source_target_pairs={{0,14},{2,0},{4,2},{6,4},{8,6},{10,8},{12,10},{14,12},{1,15},{3,1}... | collective-permute-start | bytes 442376 | tf_op jit(solution)/shard_map/ppermute | solution.py:25
  69.5 10.0 %collective-permute-start.11 = (bf16[48,1536]{1,0:T(8,128)(2,1)}, bf16[48,1536]{1,0:T(8,128)(2,1)S(1)}, u32[]{:S(2)}, u32[]{:S(2)}) collective-permute-start(bf16[48,1536]{1,0:T(8,128)(2,1)} %get-tuple-element.69.refs_0_), channel_id=1, source_target_pairs={{0,4},{2,6},{4,8},{6,10},{8,12},{10,14},{12,0},{14,2},{1,5},{3,7},... | collective-permute-start | bytes 442376 | tf_op jit(solution)/shard_map/ppermute | solution.py:25
  70.8 10.9 %collective-permute-start.9 = (bf16[48,1536]{1,0:T(8,128)(2,1)}, bf16[48,1536]{1,0:T(8,128)(2,1)S(1)}, u32[]{:S(2)}, u32[]{:S(2)}) collective-permute-start(bf16[48,1536]{1,0:T(8,128)(2,1)} %get-tuple-element.69.refs_0_), channel_id=1, source_target_pairs={{0,2},{2,4},{4,6},{6,8},{8,10},{10,12},{12,14},{14,0},{1,3},{3,5},... | collective-permute-start | bytes 442376 | tf_op jit(solution)/shard_map/ppermute | solution.py:25
  70.8 11.0 %copy-start.22 = (bf16[384,1408]{1,0:T(8,128)(2,1)S(1)}, bf16[384,1408]{1,0:T(8,128)(2,1)}, u32[]{:S(2)}) copy-start(bf16[384,1408]{1,0:T(8,128)(2,1)} %get-tuple-element.71) | copy-start | bytes 3244036
  71.6 12.4 %copy-start.17 = (bf16[48,1536]{1,0:T(8,128)(2,1)}, bf16[48,1536]{1,0:T(8,128)(2,1)S(1)}, u32[]{:S(2)}) copy-start(bf16[48,1536]{1,0:T(8,128)(2,1)S(1)} %collective-permute-done.10.refs_3_) | copy-start | bytes 442372
  77.9 6.0 %copy-start.12 = (bf16[48,1536]{1,0:T(8,128)(2,1)}, bf16[48,1536]{1,0:T(8,128)(2,1)S(1)}, u32[]{:S(2)}) copy-start(bf16[48,1536]{1,0:T(8,128)(2,1)S(1)} %collective-permute-done.8.refs_1_) | copy-start | bytes 442372
  77.9 6.9 %collective-permute-start.12 = (bf16[48,2304]{1,0:T(8,128)(2,1)S(1)}, bf16[48,2304]{1,0:T(8,128)(2,1)S(1)}, u32[]{:S(2)}, u32[]{:S(2)}) collective-permute-start(bf16[48,2304]{1,0:T(8,128)(2,1)S(1)} %pad_maximum_fusion), channel_id=1, source_target_pairs={{0,12},{2,14},{4,0},{6,2},{8,4},{10,6},{12,8},{14,10},{1,13},{3,15... | collective-permute-start | bytes 663560 | tf_op jit(solution)/shard_map/ppermute | solution.py:25
  79.5 4.4 %copy-start.18 = (bf16[48,1536]{1,0:T(8,128)(2,1)}, bf16[48,1536]{1,0:T(8,128)(2,1)S(1)}, u32[]{:S(2)}) copy-start(bf16[48,1536]{1,0:T(8,128)(2,1)S(1)} %collective-permute-done.11.refs_4_) | copy-start | bytes 442372
  81.7 2.3 %copy-start.13 = (bf16[48,1536]{1,0:T(8,128)(2,1)}, bf16[48,1536]{1,0:T(8,128)(2,1)S(1)}, u32[]{:S(2)}) copy-start(bf16[48,1536]{1,0:T(8,128)(2,1)S(1)} %collective-permute-done.9.refs_2_) | copy-start | bytes 442372
  81.7 12.1 %collective-permute-start.13 = (bf16[48,2304]{1,0:T(8,128)(2,1)S(1)}, bf16[48,2304]{1,0:T(8,128)(2,1)S(1)}, u32[]{:S(2)}, u32[]{:S(2)}) collective-permute-start(bf16[48,2304]{1,0:T(8,128)(2,1)S(1)} %pad_maximum_fusion.1), channel_id=1, source_target_pairs={{0,4},{2,6},{4,8},{6,10},{8,12},{10,14},{12,0},{14,2},{1,5},{3,7},... | collective-permute-start | bytes 663560 | tf_op jit(solution)/shard_map/ppermute | solution.py:25
  84.8 9.0 %copy-start.20 = (bf16[48,2304]{1,0:T(8,128)(2,1)}, bf16[48,2304]{1,0:T(8,128)(2,1)S(1)}, u32[]{:S(2)}) copy-start(bf16[48,2304]{1,0:T(8,128)(2,1)S(1)} %collective-permute-done.12.refs_5_) | copy-start | bytes 663556
  93.8 0.7 copy-start.21
  99.9 6.3 %collective-permute-start.16 = (bf16[48,2048]{1,0:T(8,128)(2,1)S(1)}, bf16[48,2048]{1,0:T(8,128)(2,1)S(1)}, u32[]{:S(2)}, u32[]{:S(2)}) collective-permute-start(bf16[48,2048]{1,0:T(8,128)(2,1)S(1)} %get-tuple-element.78), channel_id=1, source_target_pairs={{0,12},{2,14},{4,0},{6,2},{8,4},{10,6},{12,8},{14,10},{1,13},{3,15... | collective-permute-start | bytes 589832 | tf_op jit(solution)/shard_map/ppermute | solution.py:25
  102.8 11.8 %collective-permute-start.14 = (bf16[48,2176]{1,0:T(8,128)(2,1)S(1)}, bf16[48,2176]{1,0:T(8,128)(2,1)S(1)}, u32[]{:S(2)}, u32[]{:S(2)}) collective-permute-start(bf16[48,2176]{1,0:T(8,128)(2,1)S(1)} %get-tuple-element.76), channel_id=1, source_target_pairs={{0,4},{2,6},{4,8},{6,10},{8,12},{10,14},{12,0},{14,2},{1,5},{3,7},... | collective-permute-start | bytes 626696 | tf_op jit(solution)/shard_map/ppermute | solution.py:25
  106.3 11.1 %collective-permute-start.17 = (bf16[48,1408]{1,0:T(8,128)(2,1)S(1)}, bf16[48,1408]{1,0:T(8,128)(2,1)S(1)}, u32[]{:S(2)}, u32[]{:S(2)}) collective-permute-start(bf16[48,1408]{1,0:T(8,128)(2,1)S(1)} %add_convert_fusion), channel_id=1, source_target_pairs={{0,12},{2,14},{4,0},{6,2},{8,4},{10,6},{12,8},{14,10},{1,13},{3,15... | collective-permute-start | bytes 405512 | tf_op jit(solution)/shard_map/ppermute | solution.py:25
  109.7 7.6 %copy-start.19 = (f32[48,128]{1,0:T(8,128)S(1)}, f32[48,128]{1,0:T(8,128)}, u32[]{:S(2)}) copy-start(f32[48,128]{1,0:T(8,128)} %get-tuple-element.82) | copy-start | bytes 73732
  109.7 13.9 %copy-start.11 = (f32[48,1408]{1,0:T(8,128)S(1)}, f32[48,1408]{1,0:T(8,128)}, u32[]{:S(2)}) copy-start(f32[48,1408]{1,0:T(8,128)} %get-tuple-element.81) | copy-start | bytes 811012
  109.7 10.4 %collective-permute-start.19 = (bf16[48,1408]{1,0:T(8,128)(2,1)S(1)}, bf16[48,1408]{1,0:T(8,128)(2,1)S(1)}, u32[]{:S(2)}, u32[]{:S(2)}) collective-permute-start(bf16[48,1408]{1,0:T(8,128)(2,1)S(1)} %fusion.1), channel_id=1, source_target_pairs={{0,14},{2,0},{4,2},{6,4},{8,6},{10,8},{12,10},{14,12},{1,15},{3,1}... | collective-permute-start | bytes 405512 | tf_op jit(solution)/shard_map/ppermute | solution.py:25
  114.6 6.4 %collective-permute-start.15 = (bf16[48,1408]{1,0:T(8,128)(2,1)S(1)}, bf16[48,1408]{1,0:T(8,128)(2,1)S(1)}, u32[]{:S(2)}, u32[]{:S(2)}) collective-permute-start(bf16[48,1408]{1,0:T(8,128)(2,1)S(1)} %add_convert_fusion.1), channel_id=1, source_target_pairs={{0,4},{2,6},{4,8},{6,10},{8,12},{10,14},{12,0},{14,2},{1,5},{3,7},... | collective-permute-start | bytes 405512 | tf_op jit(solution)/shard_map/ppermute | solution.py:25
  117.1 24.0 %copy-start.7 = (f32[384,256]{1,0:T(8,128)S(1)}, f32[384,256]{1,0:T(8,128)}, u32[]{:S(2)}) copy-start(f32[384,256]{1,0:T(8,128)} %get-tuple-element.83.refs_11_) | copy-start | bytes 1179652
  117.2 23.9 %copy-start.2 = (bf16[384,3072]{1,0:T(8,128)(2,1)S(1)}, bf16[384,3072]{1,0:T(8,128)(2,1)}, u32[]{:S(2)}) copy-start(bf16[384,3072]{1,0:T(8,128)(2,1)} %refs_9_.1) | copy-start | bytes 7077892
  117.2 23.9 %copy-start.8 = (bf16[384,256]{1,0:T(8,128)(2,1)S(1)}, bf16[384,256]{1,0:T(8,128)(2,1)}, u32[]{:S(2)}) copy-start(bf16[384,256]{1,0:T(8,128)(2,1)} %get-tuple-element.84.refs_12_) | copy-start | bytes 589828
  117.2 6.4 %collective-permute-start.18 = (bf16[48,1408]{1,0:T(8,128)(2,1)S(1)}, bf16[48,1408]{1,0:T(8,128)(2,1)S(1)}, u32[]{:S(2)}, u32[]{:S(2)}) collective-permute-start(bf16[48,1408]{1,0:T(8,128)(2,1)S(1)} %fusion.2), channel_id=1, source_target_pairs={{0,2},{2,4},{4,6},{6,8},{8,10},{10,12},{12,14},{14,0},{1,3},{3,5},... | collective-permute-start | bytes 405512 | tf_op jit(solution)/shard_map/ppermute | solution.py:25
  124.0 7.1 %collective-permute-start.23 = (bf16[48,1408]{1,0:T(8,128)(2,1)S(1)}, bf16[48,1408]{1,0:T(8,128)(2,1)S(1)}, u32[]{:S(2)}, u32[]{:S(2)}) collective-permute-start(bf16[48,1408]{1,0:T(8,128)(2,1)S(1)} %multiply_convert_fusion.refs_0_), channel_id=1, source_target_pairs={{0,4},{2,6},{4,8},{6,10},{8,12},{10,14},{12,0},{14,2},{1,5},{3,7},... | collective-permute-start | bytes 405512 | tf_op jit(solution)/shard_map/ppermute | solution.py:25
  124.0 9.2 %collective-permute-start.22 = (bf16[48,1408]{1,0:T(8,128)(2,1)S(1)}, bf16[48,1408]{1,0:T(8,128)(2,1)S(1)}, u32[]{:S(2)}, u32[]{:S(2)}) collective-permute-start(bf16[48,1408]{1,0:T(8,128)(2,1)S(1)} %multiply_convert_fusion.refs_0_), channel_id=1, source_target_pairs={{0,12},{2,14},{4,0},{6,2},{8,4},{10,6},{12,8},{14,10},{1,13},{3,15... | collective-permute-start | bytes 405512 | tf_op jit(solution)/shard_map/ppermute | solution.py:25
  127.6 6.9 %collective-permute-start.21 = (bf16[48,1408]{1,0:T(8,128)(2,1)S(1)}, bf16[48,1408]{1,0:T(8,128)(2,1)S(1)}, u32[]{:S(2)}, u32[]{:S(2)}) collective-permute-start(bf16[48,1408]{1,0:T(8,128)(2,1)S(1)} %multiply_convert_fusion.refs_0_), channel_id=1, source_target_pairs={{0,2},{2,4},{4,6},{6,8},{8,10},{10,12},{12,14},{14,0},{1,3},{3,5},... | collective-permute-start | bytes 405512 | tf_op jit(solution)/shard_map/ppermute | solution.py:25
  128.2 9.6 %collective-permute-start.20 = (bf16[48,1408]{1,0:T(8,128)(2,1)S(1)}, bf16[48,1408]{1,0:T(8,128)(2,1)S(1)}, u32[]{:S(2)}, u32[]{:S(2)}) collective-permute-start(bf16[48,1408]{1,0:T(8,128)(2,1)S(1)} %multiply_convert_fusion.refs_0_), channel_id=1, source_target_pairs={{0,14},{2,0},{4,2},{6,4},{8,6},{10,8},{12,10},{14,12},{1,15},{3,1}... | collective-permute-start | bytes 405512 | tf_op jit(solution)/shard_map/ppermute | solution.py:25
  131.1 10.0 %collective-permute-start.25 = (bf16[48,1408]{1,0:T(8,128)(2,1)S(1)}, bf16[48,1408]{1,0:T(8,128)(2,1)S(1)}, u32[]{:S(2)}, u32[]{:S(2)}) collective-permute-start(bf16[48,1408]{1,0:T(8,128)(2,1)S(1)} %collective-permute-done.23.refs_4_), channel_id=1, source_target_pairs={{0,2},{2,4},{4,6},{6,8},{8,10},{10,12},{12,14},{14,0},{1,3},{3,5},... | collective-permute-start | bytes 405512 | tf_op jit(solution)/shard_map/ppermute | solution.py:25
  133.3 7.8 %collective-permute-start.24 = (bf16[48,1408]{1,0:T(8,128)(2,1)S(1)}, bf16[48,1408]{1,0:T(8,128)(2,1)S(1)}, u32[]{:S(2)}, u32[]{:S(2)}) collective-permute-start(bf16[48,1408]{1,0:T(8,128)(2,1)S(1)} %collective-permute-done.22.refs_3_), channel_id=1, source_target_pairs={{0,14},{2,0},{4,2},{6,4},{8,6},{10,8},{12,10},{14,12},{1,15},{3,1}... | collective-permute-start | bytes 405512 | tf_op jit(solution)/shard_map/ppermute | solution.py:25
  134.0 7.0 %collective-permute-start.26 = (bf16[48,768]{1,0:T(8,128)(2,1)S(1)}, bf16[48,768]{1,0:T(8,128)(2,1)S(1)}, u32[]{:S(2)}, u32[]{:S(2)}) collective-permute-start(bf16[48,768]{1,0:T(8,128)(2,1)S(1)} %slice.46), channel_id=1, source_target_pairs={{0,4},{2,6},{4,8},{6,10},{8,12},{10,14},{12,0},{14,2},{1,5},{3,7},... | collective-permute-start | bytes 221192 | tf_op jit(solution)/shard_map/ppermute | solution.py:25
  134.5 5.7 %collective-permute-start.27 = (bf16[48,640]{1,0:T(8,128)(2,1)S(1)}, bf16[48,640]{1,0:T(8,128)(2,1)S(1)}, u32[]{:S(2)}, u32[]{:S(2)}) collective-permute-start(bf16[48,640]{1,0:T(8,128)(2,1)S(1)} %slice.47), channel_id=1, source_target_pairs={{0,12},{2,14},{4,0},{6,2},{8,4},{10,6},{12,8},{14,10},{1,13},{3,15... | collective-permute-start | bytes 184328 | tf_op jit(solution)/shard_map/ppermute | solution.py:25
  141.1 15.3 %copy-start.4 = (bf16[3072,256]{1,0:T(8,128)(2,1)S(1)}, bf16[3072,256]{1,0:T(8,128)(2,1)}, u32[]{:S(2)}) copy-start(bf16[3072,256]{1,0:T(8,128)(2,1)} %w_in_ref.3) | copy-start | bytes 4718596
  145.8 13.4 %collective-permute-start.28 = (bf16[16,144,256]{2,1,0:T(8,128)(2,1)}, bf16[16,144,256]{2,1,0:T(8,128)(2,1)S(1)}, u32[]{:S(2)}, u32[]{:S(2)}) collective-permute-start(bf16[16,144,256]{2,1,0:T(8,128)(2,1)} %get-tuple-element.86), channel_id=1, source_target_pairs={{0,1},{1,0},{2,3},{3,2},{4,5},{5,4},{6,7},{7,6},{8,9},{9,8},{10,11... | collective-permute-start | bytes 3538952 | tf_op jit(solution)/shard_map/ppermute | solution.py:29
  156.4 2.8 %copy-start.6 = (bf16[16,144,256]{2,1,0:T(8,128)(2,1)S(1)}, bf16[16,144,256]{2,1,0:T(8,128)(2,1)}, u32[]{:S(2)}) copy-start(bf16[16,144,256]{2,1,0:T(8,128)(2,1)} %get-tuple-element.85.keep_ref) | copy-start | bytes 3538948
  202.1 4.9 %collective-permute-start.29 = (bf16[16,144,256]{2,1,0:T(8,128)(2,1)S(1)}, bf16[16,144,256]{2,1,0:T(8,128)(2,1)S(1)}, u32[]{:S(2)}, u32[]{:S(2)}) collective-permute-start(bf16[16,144,256]{2,1,0:T(8,128)(2,1)S(1)} %all_to_all.21.mine_ref), channel_id=1, source_target_pairs={{0,1},{1,0},{2,3},{3,2},{4,5},{5,4},{6,7},{7,6},{8,9},{9,8},{10,11... | collective-permute-start | bytes 3538952 | tf_op jit(solution)/shard_map/ppermute | solution.py:29
Sparse Core Ops, SparseCore 0:
  159.7 35.7 reduce-scatter.1
where the time goes:
time: 216 us
  starting transfers between devices  74.5 us (34%)
  waiting for transfers between devices  44.3 us (21%)
  blocking collectives  42.3 us (20%)
  Pallas kernels  27.3 us (13%)
  between operations  14.5 us (7%)
  local copies, waits for them, and re-layouts  6.17 us (3%)
  other arithmetic  4.28 us (2%)
    ppermute x28, starting transfers between devices, shift_tp(): return lax.ppermute(x, 'tp', [(i, (i + step) % NT) for i in range(NT)])  49.3 us
    ppermute x28, waiting for transfers between devices, shift_tp(): return lax.ppermute(x, 'tp', [(i, (i + step) % NT) for i in range(NT)])  41.7 us
    all_to_all x1, blocking collectives, on_device(): chip = lax.all_to_all(chip, 'seq', 0, 0, tiled=True)  22 us
    all_to_all x1, blocking collectives, to_all(): lax.all_to_all(jnp.broadcast_to(x[None], (GROUPS,) + x.shape), 'seq', 0,...  20.3 us
    ppermute x2, starting transfers between devices, swap_tea(): return lax.ppermute(x, 'tea', [(0, 1), (1, 0)])  13 us
    all_to_all x1, starting transfers between devices, on_device(): teacher_got = lax.all_to_all(teacher_send, 'seq', 0, 0, tiled=True)  7.73 us
    pallas_call x1, Pallas kernels, gram_grads(): pl.pallas_call(gram_body, out_shape=[jax.ShapeDtypeStruct(chunk.shape, ch...  5.37 us
    pallas_call x1, Pallas kernels, backward(): pl.pallas_call(backward_body, out_shape=[pltpu.HBM(halves, bf16), pltpu.H...  4.73 us
  transfers between devices with their start and end apart: 33, of which 17 were waited for; matrix products, arithmetic and copies ran while one was open for 3% of the time, Pallas kernels for 4%

commit v1 on v0

--- a/solution.py
+++ b/solution.py
@@ -41,15 +41,6 @@
     return [x, after, after2, far_after, before2, before, far_before]
 
 
-def sum_ring(own, one, two, far_after, six, seven, far_before):
-    far_after, far_before = shift_tp(far_after, 2).astype(f32), shift_tp(far_before, -2).astype(f32)
-    one, seven = one + far_after[:, :E], seven + far_before[:, :E]
-    two = two + jnp.concatenate([far_after[:, E:], jnp.zeros((SHARD, RIGHT), f32)], axis=1)
-    six = six + jnp.concatenate([jnp.zeros((SHARD, LEFT), f32), far_before[:, E:]], axis=1)
-    one, two, six, seven = (v.astype(bf16) for v in (one, two, six, seven))
-    return [shift_tp(two, 2), shift_tp(six, -2), shift_tp(one, 1), shift_tp(seven, -1)]
-
-
 def gather_split(x):
     before, after = shift_tp(x, 1), shift_tp(x, -1)
     before2, after2 = shift_tp(x, 2), shift_tp(x, -2)
@@ -106,23 +97,6 @@
 STAGE = [pltpu.VMEM((5, SHARD, E), bf16), pltpu.SemaphoreType.DMA((NT + 1,))]
 WIDE, FULL = pltpu.HBM((SHARD, E), f32), pltpu.HBM((SHARD, E), bf16)
 SPLIT = [WIDE, FULL, WIDE, FULL, pltpu.HBM((SHARD, LEFT), bf16), pltpu.HBM((SHARD, RIGHT), bf16), FULL, WIDE, FULL]
-CHUNKS = [
-    WIDE,
-    WIDE,
-    WIDE,
-    pltpu.HBM((SHARD, E + LEFT), bf16),
-    WIDE,
-    WIDE,
-    pltpu.HBM((SHARD, E + RIGHT), bf16),
-]
-
-
-def far_parts(total_ref, at, after_ref, before_ref):
-    half = total_ref[pl.ds(spot_of(at, 4), SHARD), :].astype(bf16)
-    after_ref[:, :E] = total_ref[pl.ds(spot_of(at, 3), SHARD), :].astype(bf16)
-    after_ref[:, E:] = half[:, :LEFT]
-    before_ref[:, :E] = total_ref[pl.ds(spot_of(at, 5), SHARD), :].astype(bf16)
-    before_ref[:, E:] = half[:, LEFT:]
 
 
 def chunk_out(total_ref, at, targets, stage_ref, sems):
@@ -153,9 +127,10 @@
 
 
 def chunk_store(total_ref, at, targets):
-    far_parts(total_ref, at, targets[3], targets[6])
-    for n in (0, 1, 2, 4, 5):
-        targets[n][...] = total_ref[pl.ds(spot_of(at, PLACES[n]), SHARD), :]
+    for n, target in enumerate(targets):
+        d = n if n <= 4 else n - 1
+        cols = {4: pl.ds(0, LEFT), 5: pl.ds(LEFT, RIGHT)}.get(n, pl.ds(0, E))
+        target[...] = total_ref[pl.ds(spot_of(at, d), SHARD), cols].astype(target.dtype)
 
 
 def align_body(at_ref, teacher_hbm, patch_ref, picks_ref, rows_hbm, send_hbm, teacher_ref, rows_ref, own_ref, extra_ref, sems):
@@ -345,8 +320,8 @@
     pieces, refs = dict(zip(PIECE_ORDER, refs[:PARTS])), refs[PARTS:]
     keys_hbm, teacher_hbm, spread_ref = refs[:3]
     refs = refs[3:]
-    targets = refs[:PARTS]
-    row_ref, key_ref, teacher_ref, grad_ref, total_ref, sems = refs[PARTS:]
+    targets = refs[: NT + 1]
+    row_ref, key_ref, teacher_ref, grad_ref, total_ref, sems = refs[NT + 1 :]
     contract = (((1,), (1,)), ((), ()))
     step = 256
     spans = [pl.ds(k, step) for k in range(0, GROUPS * SHARD, step)]
@@ -388,9 +363,9 @@
     steps = GROUPS * SHARD // 256
     return pl.pallas_call(
         gram_body,
-        out_shape=[jax.ShapeDtypeStruct(chunk.shape, chunk.dtype) for chunk in CHUNKS],
+        out_shape=[jax.ShapeDtypeStruct(chunk.shape, chunk.dtype) for chunk in SPLIT],
         in_specs=[IN_SMEM] + in_place(PARTS + 2) + in_vmem(1),
-        out_specs=in_vmem(PARTS),
+        out_specs=in_vmem(NT + 1),
         scratch_shapes=[
             pltpu.VMEM((ROWS, E_WIDE), bf16),
             pltpu.VMEM((GROUPS * SHARD, E), bf16),
@@ -650,7 +625,7 @@
 
     row_grad = gram_grads(at, rows, keys, gram_teacher, spread)
     unit_grad = row_grad[0]
-    for piece in sum_ring(*row_grad):
+    for piece in sum_split(*row_grad):
         unit_grad = unit_grad + piece.astype(f32)
     inner = jnp.sum(unit_student * unit_grad, axis=-1, keepdims=True)
     grad_proj = ((unit_grad - unit_student * inner) * inv_norm).astype(bf16)

time: 216 us -> 215 us (level)
  starting transfers between devices: 74.5 us -> 68.2 us
  waiting for transfers between devices: 44.3 us -> 50.3 us
    ppermute x28 -> x30, waiting for transfers between devices: 41.7 us -> 47.7 us  [shift_tp(): return lax.ppermute(x, 'tp', [(i, (i + step) % NT) for i in range(NT)])]
    ppermute x28 -> x30, starting transfers between devices: 49.3 us -> 43.3 us  [shift_tp(): return lax.ppermute(x, 'tp', [(i, (i + step) % NT) for i in range(NT)])]
  transfers between devices with their start and end apart: 33 -> 35, of which waited for: 17 -> 16; matrix products, arithmetic and copies ran while one was open for 3% -> 3% of each run, Pallas kernels for 4% -> 4%
where the time goes in v1:
time: 215 us; the launch traced here: 214 us
  starting transfers between devices  68.2 us (32%)
  waiting for transfers between devices  50.3 us (23%)
  blocking collectives  41.7 us (19%)
  Pallas kernels  27.4 us (13%)
  between operations  14.5 us (7%)
  local copies, waits for them, and re-layouts  6.14 us (3%)
  other arithmetic  4.16 us (2%)
    ppermute x30, waiting for transfers between devices, shift_tp(): return lax.ppermute(x, 'tp', [(i, (i + step) % NT) for i in range(NT)])  47.7 us
    ppermute x30, starting transfers between devices, shift_tp(): return lax.ppermute(x, 'tp', [(i, (i + step) % NT) for i in range(NT)])  43.3 us
    all_to_all x1, blocking collectives, on_device(): chip = lax.all_to_all(chip, 'seq', 0, 0, tiled=True)  21.4 us
    all_to_all x1, blocking collectives, to_all(): lax.all_to_all(jnp.broadcast_to(x[None], (GROUPS,) + x.shape), 'seq', 0,...  20.2 us
    ppermute x2, starting transfers between devices, swap_tea(): return lax.ppermute(x, 'tea', [(0, 1), (1, 0)])  12.6 us
    all_to_all x1, starting transfers between devices, on_device(): teacher_got = lax.all_to_all(teacher_send, 'seq', 0, 0, tiled=True)  7.73 us
    pallas_call x1, Pallas kernels, gram_grads(): pl.pallas_call(gram_body, out_shape=[jax.ShapeDtypeStruct(chunk.shape, ch...  5.36 us
    pallas_call x1, Pallas kernels, backward(): pl.pallas_call(backward_body, out_shape=[pltpu.HBM(halves, bf16), pltpu.H...  4.76 us
  transfers between devices with their start and end apart: 35, of which 16 were waited for; matrix products, arithmetic and copies ran while one was open for 3% of the time, Pallas kernels for 4%

profile of v1, /device:TPU:1, one launch (start us, length us, event | category | flops | bytes accessed | tf_op | source)
XLA Modules:
  0.0 214.5 jit_solution(11967134742259063541)
XLA Ops:
  7.2 0.7 reshape.63.patch_ref
  7.9 0.7 copy-done.9
  8.6 4.1 %align.1 = (bf16[384,1408]{1,0:T(8,128)(2,1)}, bf16[16,48,1536]{2,1,0:T(8,128)(2,1)}) custom-call(s32[2]{0:T(128)S(1)} %pad_add_fusion.2.at_ref, bf16[192,1408]{1,0:T(8,128)(2,1)} %teacher_hbm.1, s32[1,384]{1,0:T(1,128)S(1)} %reshape.63.patch_ref, s32[16]{0:T(128)S(1)} %bitcast.12), custom_call_target="tpu_custom_call" | custom-call | flops 250000000 | bytes 4000000 | tf_op jit(solution)/shard_map/align/pallas_call | solution.py:163
  12.8 7.7 %all-to-all-start = ((bf16[16,48,1536]{2,1,0:T(8,128)(2,1)}), bf16[16,48,1536]{2,1,0:T(8,128)(2,1)S(1)}, u32[]{:S(2)}, u32[]{:S(2)}) async-start(bf16[16,48,1536]{2,1,0:T(8,128)(2,1)} %get-tuple-element.65), calls=%async_computation | async-start | bytes 4718592 | tf_op jit(solution)/shard_map/all_to_all | solution.py:602
  20.5 1.7 copy-done.1
  22.2 1.4 copy-done.3
  23.6 2.9 %forward.1 = (f32[384,256]{1,0:T(8,128)}, bf16[384,256]{1,0:T(8,128)(2,1)}, f32[48,1408]{1,0:T(8,128)}, bf16[48,1408]{1,0:T(8,128)(2,1)}, f32[48,1408]{1,0:T(8,1...) custom-call(s32[1]{0:T(128)} %bitcast.1.at_ref, ...), custom_call_target="tpu_custom_call" | custom-call | flops 900000000 | bytes 8000000 | tf_op jit(solution)/shard_map/forward/pallas_call | solution.py:205
  26.5 1.7 collective-permute-start.2
  28.2 3.0 %collective-permute-start.3 = (bf16[48,768]{1,0:T(8,128)(2,1)}, bf16[48,768]{1,0:T(8,128)(2,1)}, u32[]{:S(2)}, u32[]{:S(2)}) collective-permute-start(bf16[48,768]{1,0:T(8,128)(2,1)} %get-tuple-element.61), channel_id=1, source_target_pairs={{0,4},{2,6},{4,8},{6,10},{8,12},{10,14},{12,0},{14,2},{1,5},{3,7},... | collective-permute-start | bytes 221192 | tf_op jit(solution)/shard_map/ppermute | solution.py:25
  31.2 2.1 collective-permute-start.6
  33.4 0.7 collective-permute-start
  34.1 2.0 collective-permute-start.1
  36.0 2.3 %collective-permute-done.3 = bf16[48,768]{1,0:T(8,128)(2,1)} collective-permute-done((bf16[48,768]{1,0:T(8,128)(2,1)}, bf16[48,768]{1,0:T(8,128)(2,1)}, u32[]{:S(2)}, u32[]{:S(2)}) %collective-permute-start.3) | collective-permute-done | bytes 73760 | tf_op jit(solution)/shard_map/ppermute | solution.py:25
  38.3 1.0 collective-permute-start.5
  39.3 1.7 add_convert_fusion.3
  41.0 0.4 collective-permute-start.4
  41.4 1.3 collective-permute-done.5
  42.7 1.7 add_convert_fusion.2
  44.4 2.0 collective-permute-start.7
  46.4 0.4 dynamic-slice_reduce_fusion
  47.1 0.3 collective-permute-done.4.refs_2_
  47.4 5.1 %collective-permute-done.7.refs_3_ = bf16[48,1408]{1,0:T(8,128)(2,1)} collective-permute-done((bf16[48,1408]{1,0:T(8,128)(2,1)}, bf16[48,1408]{1,0:T(8,128)(2,1)}, u32[]{:S(2)}, u32[]{:S(2)}) %collective-permute-start.7) | collective-permute-done | bytes 135200 | tf_op jit(solution)/shard_map/ppermute | solution.py:25
  52.5 2.6 %all-to-all-done.theirs_hbm = bf16[16,48,1536]{2,1,0:T(8,128)(2,1)S(1)} async-done(((bf16[16,48,1536]{2,1,0:T(8,128)(2,1)}), bf16[16,48,1536]{2,1,0:T(8,128)(2,1)S(1)}, u32[]{:S(2)}, u32[]{:S(2)}) %all-to-all-start) | async-done | bytes 2359328 | tf_op jit(solution)/shard_map/all_to_all | solution.py:602
  55.1 3.0 %normalise.1 = (f32[48,1408]{1,0:T(8,128)}, f32[48,128]{1,0:T(8,128)}, bf16[48,1536]{1,0:T(8,128)(2,1)}, bf16[16,48,1408]{2,1,0:T(8,128)(2,1)}) custom-call(s32[8,128]{1,0:T(8,128)S(1)} %pad.12.local_ref, f32[48,1408]{1,0:T(8,128)} %get-tuple-element.56.own_hbm, bf16[16,48,1536]{2,1,0:T(8,128)(2,1)S(1)} %all-to-all-done.theirs_hbm, ...), custom_call_target="tpu_custom_call" | custom-call | flops 1000000 | bytes 4000000 | tf_op jit(solution)/shard_map/normalise/pallas_call | solution.py:277
  58.1 4.5 %all-to-all-start.1 = ((bf16[16,48,1408]{2,1,0:T(8,128)(2,1)}), bf16[16,48,1408]{2,1,0:T(8,128)(2,1)}, u32[]{:S(2)}, u32[]{:S(2)}) async-start(bf16[16,48,1408]{2,1,0:T(8,128)(2,1)} %get-tuple-element.72), calls=%async_computation.1 | async-start | bytes 4325376 | tf_op jit(solution)/shard_map/all_to_all | solution.py:620
  62.7 6.1 %collective-permute-start.10 = (bf16[48,1536]{1,0:T(8,128)(2,1)}, bf16[48,1536]{1,0:T(8,128)(2,1)S(1)}, u32[]{:S(2)}, u32[]{:S(2)}) collective-permute-start(bf16[48,1536]{1,0:T(8,128)(2,1)} %get-tuple-element.71.refs_0_), channel_id=1, source_target_pairs={{0,12},{2,14},{4,0},{6,2},{8,4},{10,6},{12,8},{14,10},{1,13},{3,15... | collective-permute-start | bytes 442376 | tf_op jit(solution)/shard_map/ppermute | solution.py:25
  68.8 0.7 collective-permute-start.8
  69.5 1.3 collective-permute-start.11
  71.0 0.6 collective-permute-done.10.refs_3_
  71.6 6.3 %collective-permute-done.8.refs_1_ = bf16[48,1536]{1,0:T(8,128)(2,1)S(1)} collective-permute-done((bf16[48,1536]{1,0:T(8,128)(2,1)}, bf16[48,1536]{1,0:T(8,128)(2,1)S(1)}, u32[]{:S(2)}, u32[]{:S(2)}) %collective-permute-start.8) | collective-permute-done | bytes 147488 | tf_op jit(solution)/shard_map/ppermute | solution.py:25
  77.9 1.6 collective-permute-start.12
  79.6 2.1 collective-permute-done.9.refs_2_
  81.8 2.1 fusion.16.refs_8_
  83.9 0.9 collective-permute-done.12.refs_5_
  84.9 8.8 %collective-permute-done.13.refs_6_ = bf16[48,2304]{1,0:T(8,128)(2,1)S(1)} collective-permute-done((bf16[48,2304]{1,0:T(8,128)(2,1)S(1)}, bf16[48,2304]{1,0:T(8,128)(2,1)S(1)}, u32[]{:S(2)}, u32[]{:S(2)}) %collective-permute-start.13) | collective-permute-done | bytes 221216 | tf_op jit(solution)/shard_map/ppermute | solution.py:25
  93.7 0.7 copy-done.21
  94.4 5.4 %gram_grads.1 = (f32[48,1408]{1,0:T(8,128)S(1)}, bf16[48,1408]{1,0:T(8,128)(2,1)S(1)}, f32[48,1408]{1,0:T(8,128)S(1)}, bf16[48,1408]{1,0:T(8,128)(2,1)S(1)}, bf1...) custom-call(s32[1]{0:T(128)} %bitcast.1.at_ref, ...), custom_call_target="tpu_custom_call" | custom-call | flops 1700000000 | bytes 9000000 | tf_op jit(solution)/shard_map/gram_grads/pallas_call | solution.py:364
  99.8 1.4 collective-permute-start.17
  101.3 2.3 %collective-permute-start.20 = (bf16[48,640]{1,0:T(8,128)(2,1)S(1)}, bf16[48,640]{1,0:T(8,128)(2,1)S(1)}, u32[]{:S(2)}, u32[]{:S(2)}) collective-permute-start(bf16[48,640]{1,0:T(8,128)(2,1)S(1)} %get-tuple-element.84), channel_id=1, source_target_pairs={{0,12},{2,14},{4,0},{6,2},{8,4},{10,6},{12,8},{14,10},{1,13},{3,15... | collective-permute-start | bytes 184328 | tf_op jit(solution)/shard_map/ppermute | solution.py:25
  103.6 0.7 collective-permute-start.14
  104.3 2.0 collective-permute-start.15
  106.3 1.1 collective-permute-done.17
  107.3 1.1 collective-permute-start.19
  108.5 4.9 %collective-permute-done.19 = bf16[48,1408]{1,0:T(8,128)(2,1)S(1)} collective-permute-done((bf16[48,1408]{1,0:T(8,128)(2,1)S(1)}, bf16[48,1408]{1,0:T(8,128)(2,1)S(1)}, u32[]{:S(2)}, u32[]{:S(2)}) %collective-permute-start.19) | collective-permute-done | bytes 135200 | tf_op jit(solution)/shard_map/ppermute | solution.py:25
  113.5 0.6 collective-permute-start.21
  114.2 2.3 %collective-permute-done.18 = bf16[48,1408]{1,0:T(8,128)(2,1)S(1)} collective-permute-done((bf16[48,1408]{1,0:T(8,128)(2,1)S(1)}, bf16[48,1408]{1,0:T(8,128)(2,1)S(1)}, u32[]{:S(2)}, u32[]{:S(2)}) %collective-permute-start.18) | collective-permute-done | bytes 135200 | tf_op jit(solution)/shard_map/ppermute | solution.py:25
  116.6 4.4 %collective-permute-done.21 = bf16[48,1408]{1,0:T(8,128)(2,1)S(1)} collective-permute-done((bf16[48,1408]{1,0:T(8,128)(2,1)S(1)}, bf16[48,1408]{1,0:T(8,128)(2,1)S(1)}, u32[]{:S(2)}, u32[]{:S(2)}) %collective-permute-start.21) | collective-permute-done | bytes 135200 | tf_op jit(solution)/shard_map/ppermute | solution.py:25
  121.4 0.4 collective-permute-start.25
  121.8 3.2 %collective-permute-start.24 = (bf16[48,1408]{1,0:T(8,128)(2,1)S(1)}, bf16[48,1408]{1,0:T(8,128)(2,1)S(1)}, u32[]{:S(2)}, u32[]{:S(2)}) collective-permute-start(bf16[48,1408]{1,0:T(8,128)(2,1)S(1)} %multiply_convert_fusion.refs_0_), channel_id=1, source_target_pairs={{0,12},{2,14},{4,0},{6,2},{8,4},{10,6},{12,8},{14,10},{1,13},{3,15... | collective-permute-start | bytes 405512 | tf_op jit(solution)/shard_map/ppermute | solution.py:25
  125.0 2.7 %collective-permute-start.22 = (bf16[48,1408]{1,0:T(8,128)(2,1)S(1)}, bf16[48,1408]{1,0:T(8,128)(2,1)S(1)}, u32[]{:S(2)}, u32[]{:S(2)}) collective-permute-start(bf16[48,1408]{1,0:T(8,128)(2,1)S(1)} %multiply_convert_fusion.refs_0_), channel_id=1, source_target_pairs={{0,14},{2,0},{4,2},{6,4},{8,6},{10,8},{12,10},{14,12},{1,15},{3,1}... | collective-permute-start | bytes 405512 | tf_op jit(solution)/shard_map/ppermute | solution.py:25
  127.7 1.6 collective-permute-done.24.refs_3_
  129.3 2.4 %collective-permute-start.26 = (bf16[48,1408]{1,0:T(8,128)(2,1)S(1)}, bf16[48,1408]{1,0:T(8,128)(2,1)S(1)}, u32[]{:S(2)}, u32[]{:S(2)}) collective-permute-start(bf16[48,1408]{1,0:T(8,128)(2,1)S(1)} %collective-permute-done.24.refs_3_), channel_id=1, source_target_pairs={{0,14},{2,0},{4,2},{6,4},{8,6},{10,8},{12,10},{14,12},{1,15},{3,1}... | collective-permute-start | bytes 405512 | tf_op jit(solution)/shard_map/ppermute | solution.py:25
  131.7 0.4 collective-permute-start.28
  132.1 3.2 %collective-permute-start.29 = (bf16[48,640]{1,0:T(8,128)(2,1)S(1)}, bf16[48,640]{1,0:T(8,128)(2,1)S(1)}, u32[]{:S(2)}, u32[]{:S(2)}) collective-permute-start(bf16[48,640]{1,0:T(8,128)(2,1)S(1)} %slice.27), channel_id=1, source_target_pairs={{0,12},{2,14},{4,0},{6,2},{8,4},{10,6},{12,8},{14,10},{1,13},{3,15... | collective-permute-start | bytes 184328 | tf_op jit(solution)/shard_map/ppermute | solution.py:25
  135.5 5.5 %collective-permute-done.29.refs_8_ = bf16[48,640]{1,0:T(8,128)(2,1)S(1)} collective-permute-done((bf16[48,640]{1,0:T(8,128)(2,1)S(1)}, bf16[48,640]{1,0:T(8,128)(2,1)S(1)}, u32[]{:S(2)}, u32[]{:S(2)}) %collective-permute-start.29) | collective-permute-done | bytes 61472 | tf_op jit(solution)/shard_map/ppermute | solution.py:25
  141.0 4.8 %backward.1 = (bf16[16,144,256]{2,1,0:T(8,128)(2,1)}, bf16[16,144,256]{2,1,0:T(8,128)(2,1)}, bf16[384,256]{1,0:T(8,128)(2,1)}) custom-call(s32[2]{0:T(128)S(1)} %pad_add_fusion.1.at_ref, bf16[48,1408]{1,0:T(8,128)(2,1)S(1)} %multiply_convert_fusion.refs_0_, bf16[48,1408]{1,0:T(8,128)(2,1)S(1)} %collective-permute-done.22.refs_1_, ...), custom_call_target="tpu_custom_call" | custom-call | flops 1200000000 | bytes 9000000 | tf_op jit(solution)/shard_map/backward/pallas_call | solution.py:437
  145.7 10.2 %collective-permute-start.30 = (bf16[16,144,256]{2,1,0:T(8,128)(2,1)}, bf16[16,144,256]{2,1,0:T(8,128)(2,1)S(1)}, u32[]{:S(2)}, u32[]{:S(2)}) collective-permute-start(bf16[16,144,256]{2,1,0:T(8,128)(2,1)} %get-tuple-element.90), channel_id=1, source_target_pairs={{0,1},{1,0},{2,3},{3,2},{4,5},{5,4},{6,7},{7,6},{8,9},{9,8},{10,11... | collective-permute-start | bytes 3538952 | tf_op jit(solution)/shard_map/ppermute | solution.py:29
  156.0 2.8 %hidden_grads.1 = bf16[3072,384]{1,0:T(8,128)(2,1)} custom-call(bf16[384,256]{1,0:T(8,128)(2,1)} %get-tuple-element.91.grad_pre_hbm, bf16[3072,256]{1,0:T(8,128)(2,1)S(1)} %copy-done.4), custom_call_target="tpu_custom_call" | custom-call | flops 600000000 | bytes 4000000 | tf_op jit(solution)/shard_map/hidden_grads/pallas_call | solution.py:479
  158.8 0.3 pair_sum.1
  159.1 21.4 %all_to_all.20 = bf16[16,144,256]{2,1,0:T(8,128)(2,1)S(1)} all-to-all(bf16[16,144,256]{2,1,0:T(8,128)(2,1)S(1)} %pair_sum.1), channel_id=1, replica_groups=mesh['seq'=16,'tp'=8,'tea'=2] {'seq'}, dimensions={0} | all-to-all | bytes 2359296 | tf_op jit(solution)/shard_map/all_to_all | solution.py:640
  180.8 20.2 %all_to_all.21.mine_ref = bf16[16,144,256]{2,1,0:T(8,128)(2,1)S(1)} all-to-all(bf16[16,144,256]{2,1,0:T(8,128)(2,1)S(1)} %broadcast_in_dim.25), channel_id=1, replica_groups=mesh['seq'=16,'tp'=8,'tea'=2] {'seq'}, dimensions={0} | all-to-all | bytes 2359296 | tf_op jit(solution)/shard_map/all_to_all | solution.py:68
  201.0 2.4 %collective-permute-start.31 = (bf16[16,144,256]{2,1,0:T(8,128)(2,1)S(1)}, bf16[16,144,256]{2,1,0:T(8,128)(2,1)S(1)}, u32[]{:S(2)}, u32[]{:S(2)}) collective-permute-start(bf16[16,144,256]{2,1,0:T(8,128)(2,1)S(1)} %all_to_all.21.mine_ref), channel_id=1, source_target_pairs={{0,1},{1,0},{2,3},{3,2},{4,5},{5,4},{6,7},{7,6},{8,9},{9,8},{10,11... | collective-permute-start | bytes 3538952 | tf_op jit(solution)/shard_map/ppermute | solution.py:29
  203.5 2.5 %first_half.1 = (f32[3072,256]{1,0:T(8,128)}, f32[256,1408]{1,0:T(8,128)}, f32[384,384]{1,0:T(8,128)}) custom-call(s32[1]{0:T(128)} %bitcast.tea_ref, bf16[16,144,256]{2,1,0:T(8,128)(2,1)S(1)} %all_to_all.21.mine_ref, bf16[384,384]{1,0:T(8,128)(2,1)} %reduce-scatter.2.cloned.1.call-done.sum_hbm), custom_call_target="tpu_custom_call" | custom-call | bytes 5000000 | tf_op jit(solution)/shard_map/first_half/pallas_call | solution.py:559
  206.0 1.7 second_half.1
  (92 shorter events, 1.8 us)
Async XLA Ops:
  7.2 39.2 %copy-start = (s32[16,1,1,16]{3,2,1,0:T(1,128)S(1)}, s32[16,1,1,16]{3,2,1,0:T(1,128)}, u32[]{:S(2)}) copy-start(s32[16,1,1,16]{3,2,1,0:T(1,128)} %param.13) | copy-start | bytes 3076
  7.9 0.7 copy-start.9
  12.7 7.8 %copy-start.5 = (bf16[256,1408]{1,0:T(8,128)(2,1)S(1)}, bf16[256,1408]{1,0:T(8,128)(2,1)}, u32[]{:S(2)}) copy-start(bf16[256,1408]{1,0:T(8,128)(2,1)} %refs_10_.1) | copy-start | bytes 2162692
  12.8 42.4 %all-to-all-start = ((bf16[16,48,1536]{2,1,0:T(8,128)(2,1)}), bf16[16,48,1536]{2,1,0:T(8,128)(2,1)S(1)}, u32[]{:S(2)}, u32[]{:S(2)}) async-start(bf16[16,48,1536]{2,1,0:T(8,128)(2,1)} %get-tuple-element.65), calls=%async_computation | async-start | bytes 4718592 | tf_op jit(solution)/shard_map/all_to_all | solution.py:602
  20.5 1.7 copy-start.1
  22.2 1.4 copy-start.3
  23.6 23.2 %copy-start.10 = (s32[1,1,1,16]{3,2,1,0:T(1,128)S(1)}, s32[1,1,1,16]{3,2,1,0:T(1,128)}, u32[]{:S(2)}) copy-start(s32[1,1,1,16]{3,2,1,0:T(1,128)} %param.12) | copy-start | bytes 196
  26.5 12.8 %collective-permute-start.2 = (bf16[48,1408]{1,0:T(8,128)(2,1)}, bf16[48,1408]{1,0:T(8,128)(2,1)S(1)}, u32[]{:S(2)}, u32[]{:S(2)}) collective-permute-start(bf16[48,1408]{1,0:T(8,128)(2,1)} %get-tuple-element.60), channel_id=1, source_target_pairs={{0,2},{2,4},{4,6},{6,8},{8,10},{10,12},{12,14},{14,0},{1,3},{3,5},... | collective-permute-start | bytes 405512 | tf_op jit(solution)/shard_map/ppermute | solution.py:25
  28.2 10.1 %collective-permute-start.3 = (bf16[48,768]{1,0:T(8,128)(2,1)}, bf16[48,768]{1,0:T(8,128)(2,1)}, u32[]{:S(2)}, u32[]{:S(2)}) collective-permute-start(bf16[48,768]{1,0:T(8,128)(2,1)} %get-tuple-element.61), channel_id=1, source_target_pairs={{0,4},{2,6},{4,8},{6,10},{8,12},{10,14},{12,0},{14,2},{1,5},{3,7},... | collective-permute-start | bytes 221192 | tf_op jit(solution)/shard_map/ppermute | solution.py:25
  31.2 10.2 %collective-permute-start.6 = (bf16[48,640]{1,0:T(8,128)(2,1)}, bf16[48,640]{1,0:T(8,128)(2,1)}, u32[]{:S(2)}, u32[]{:S(2)}) collective-permute-start(bf16[48,640]{1,0:T(8,128)(2,1)} %get-tuple-element.64), channel_id=1, source_target_pairs={{0,12},{2,14},{4,0},{6,2},{8,4},{10,6},{12,8},{14,10},{1,13},{3,15... | collective-permute-start | bytes 184328 | tf_op jit(solution)/shard_map/ppermute | solution.py:25
  33.4 13.7 %collective-permute-start = (bf16[48,1408]{1,0:T(8,128)(2,1)}, bf16[48,1408]{1,0:T(8,128)(2,1)S(1)}, u32[]{:S(2)}, u32[]{:S(2)}) collective-permute-start(bf16[48,1408]{1,0:T(8,128)(2,1)} %get-tuple-element.57), channel_id=1, source_target_pairs={{0,2},{2,4},{4,6},{6,8},{8,10},{10,12},{12,14},{14,0},{1,3},{3,5},... | collective-permute-start | bytes 405512 | tf_op jit(solution)/shard_map/ppermute | solution.py:25
  34.1 13.0 %collective-permute-start.1 = (bf16[48,1408]{1,0:T(8,128)(2,1)}, bf16[48,1408]{1,0:T(8,128)(2,1)S(1)}, u32[]{:S(2)}, u32[]{:S(2)}) collective-permute-start(bf16[48,1408]{1,0:T(8,128)(2,1)} %get-tuple-element.58), channel_id=1, source_target_pairs={{0,14},{2,0},{4,2},{6,4},{8,6},{10,8},{12,10},{14,12},{1,15},{3,1}... | collective-permute-start | bytes 405512 | tf_op jit(solution)/shard_map/ppermute | solution.py:25
  38.3 4.4 %collective-permute-start.5 = (bf16[48,1408]{1,0:T(8,128)(2,1)}, bf16[48,1408]{1,0:T(8,128)(2,1)S(1)}, u32[]{:S(2)}, u32[]{:S(2)}) collective-permute-start(bf16[48,1408]{1,0:T(8,128)(2,1)} %get-tuple-element.63), channel_id=1, source_target_pairs={{0,14},{2,0},{4,2},{6,4},{8,6},{10,8},{12,10},{14,12},{1,15},{3,1}... | collective-permute-start | bytes 405512 | tf_op jit(solution)/shard_map/ppermute | solution.py:25
  41.0 6.4 %collective-permute-start.4 = (bf16[48,1408]{1,0:T(8,128)(2,1)}, bf16[48,1408]{1,0:T(8,128)(2,1)S(1)}, u32[]{:S(2)}, u32[]{:S(2)}) collective-permute-start(bf16[48,1408]{1,0:T(8,128)(2,1)} %add_convert_fusion.3), channel_id=1, source_target_pairs={{0,4},{2,6},{4,8},{6,10},{8,12},{10,14},{12,0},{14,2},{1,5},{3,7},... | collective-permute-start | bytes 405512 | tf_op jit(solution)/shard_map/ppermute | solution.py:25
  44.4 8.1 %collective-permute-start.7 = (bf16[48,1408]{1,0:T(8,128)(2,1)}, bf16[48,1408]{1,0:T(8,128)(2,1)}, u32[]{:S(2)}, u32[]{:S(2)}) collective-permute-start(bf16[48,1408]{1,0:T(8,128)(2,1)} %add_convert_fusion.2), channel_id=1, source_target_pairs={{0,12},{2,14},{4,0},{6,2},{8,4},{10,6},{12,8},{14,10},{1,13},{3,15... | collective-permute-start | bytes 405512 | tf_op jit(solution)/shard_map/ppermute | solution.py:25
  47.0 8.1 %copy-start.14 = (bf16[48,1408]{1,0:T(8,128)(2,1)}, bf16[48,1408]{1,0:T(8,128)(2,1)S(1)}, u32[]{:S(2)}) copy-start(bf16[48,1408]{1,0:T(8,128)(2,1)S(1)} %collective-permute-done.refs_0_) | copy-start | bytes 405508
  47.0 8.1 %copy-start.15 = (bf16[48,1408]{1,0:T(8,128)(2,1)}, bf16[48,1408]{1,0:T(8,128)(2,1)S(1)}, u32[]{:S(2)}) copy-start(bf16[48,1408]{1,0:T(8,128)(2,1)S(1)} %collective-permute-done.1.refs_1_) | copy-start | bytes 405508
  47.4 7.8 %copy-start.16 = (bf16[48,1408]{1,0:T(8,128)(2,1)}, bf16[48,1408]{1,0:T(8,128)(2,1)S(1)}, u32[]{:S(2)}) copy-start(bf16[48,1408]{1,0:T(8,128)(2,1)S(1)} %collective-permute-done.4.refs_2_) | copy-start | bytes 405508
  58.1 35.6 %all-to-all-start.1 = ((bf16[16,48,1408]{2,1,0:T(8,128)(2,1)}), bf16[16,48,1408]{2,1,0:T(8,128)(2,1)}, u32[]{:S(2)}, u32[]{:S(2)}) async-start(bf16[16,48,1408]{2,1,0:T(8,128)(2,1)} %get-tuple-element.72), calls=%async_computation.1 | async-start | bytes 4325376 | tf_op jit(solution)/shard_map/all_to_all | solution.py:620
  62.6 140.9 %reduce-scatter.2.cloned.1.call-start = ((), (), s32[]{:S(2)}) async-start(), calls=%async_computation.5 | async-start | bytes 2654208 | tf_op jit(solution)/shard_map/reduce_scatter | solution.py:639
  62.7 8.9 %collective-permute-start.10 = (bf16[48,1536]{1,0:T(8,128)(2,1)}, bf16[48,1536]{1,0:T(8,128)(2,1)S(1)}, u32[]{:S(2)}, u32[]{:S(2)}) collective-permute-start(bf16[48,1536]{1,0:T(8,128)(2,1)} %get-tuple-element.71.refs_0_), channel_id=1, source_target_pairs={{0,12},{2,14},{4,0},{6,2},{8,4},{10,6},{12,8},{14,10},{1,13},{3,15... | collective-permute-start | bytes 442376 | tf_op jit(solution)/shard_map/ppermute | solution.py:25
  68.8 9.2 %collective-permute-start.8 = (bf16[48,1536]{1,0:T(8,128)(2,1)}, bf16[48,1536]{1,0:T(8,128)(2,1)S(1)}, u32[]{:S(2)}, u32[]{:S(2)}) collective-permute-start(bf16[48,1536]{1,0:T(8,128)(2,1)} %get-tuple-element.71.refs_0_), channel_id=1, source_target_pairs={{0,14},{2,0},{4,2},{6,4},{8,6},{10,8},{12,10},{14,12},{1,15},{3,1}... | collective-permute-start | bytes 442376 | tf_op jit(solution)/shard_map/ppermute | solution.py:25
  69.5 10.0 %collective-permute-start.11 = (bf16[48,1536]{1,0:T(8,128)(2,1)}, bf16[48,1536]{1,0:T(8,128)(2,1)S(1)}, u32[]{:S(2)}, u32[]{:S(2)}) collective-permute-start(bf16[48,1536]{1,0:T(8,128)(2,1)} %get-tuple-element.71.refs_0_), channel_id=1, source_target_pairs={{0,4},{2,6},{4,8},{6,10},{8,12},{10,14},{12,0},{14,2},{1,5},{3,7},... | collective-permute-start | bytes 442376 | tf_op jit(solution)/shard_map/ppermute | solution.py:25
  70.8 10.9 %collective-permute-start.9 = (bf16[48,1536]{1,0:T(8,128)(2,1)}, bf16[48,1536]{1,0:T(8,128)(2,1)S(1)}, u32[]{:S(2)}, u32[]{:S(2)}) collective-permute-start(bf16[48,1536]{1,0:T(8,128)(2,1)} %get-tuple-element.71.refs_0_), channel_id=1, source_target_pairs={{0,2},{2,4},{4,6},{6,8},{8,10},{10,12},{12,14},{14,0},{1,3},{3,5},... | collective-permute-start | bytes 442376 | tf_op jit(solution)/shard_map/ppermute | solution.py:25
  70.8 11.0 %copy-start.22 = (bf16[384,1408]{1,0:T(8,128)(2,1)S(1)}, bf16[384,1408]{1,0:T(8,128)(2,1)}, u32[]{:S(2)}) copy-start(bf16[384,1408]{1,0:T(8,128)(2,1)} %get-tuple-element.73) | copy-start | bytes 3244036
  71.6 12.4 %copy-start.17 = (bf16[48,1536]{1,0:T(8,128)(2,1)}, bf16[48,1536]{1,0:T(8,128)(2,1)S(1)}, u32[]{:S(2)}) copy-start(bf16[48,1536]{1,0:T(8,128)(2,1)S(1)} %collective-permute-done.10.refs_3_) | copy-start | bytes 442372
  77.9 6.0 %copy-start.12 = (bf16[48,1536]{1,0:T(8,128)(2,1)}, bf16[48,1536]{1,0:T(8,128)(2,1)S(1)}, u32[]{:S(2)}) copy-start(bf16[48,1536]{1,0:T(8,128)(2,1)S(1)} %collective-permute-done.8.refs_1_) | copy-start | bytes 442372
  77.9 6.9 %collective-permute-start.12 = (bf16[48,2304]{1,0:T(8,128)(2,1)S(1)}, bf16[48,2304]{1,0:T(8,128)(2,1)S(1)}, u32[]{:S(2)}, u32[]{:S(2)}) collective-permute-start(bf16[48,2304]{1,0:T(8,128)(2,1)S(1)} %pad_maximum_fusion), channel_id=1, source_target_pairs={{0,12},{2,14},{4,0},{6,2},{8,4},{10,6},{12,8},{14,10},{1,13},{3,15... | collective-permute-start | bytes 663560 | tf_op jit(solution)/shard_map/ppermute | solution.py:25
  79.6 4.4 %copy-start.18 = (bf16[48,1536]{1,0:T(8,128)(2,1)}, bf16[48,1536]{1,0:T(8,128)(2,1)S(1)}, u32[]{:S(2)}) copy-start(bf16[48,1536]{1,0:T(8,128)(2,1)S(1)} %collective-permute-done.11.refs_4_) | copy-start | bytes 442372
  81.7 2.3 %copy-start.13 = (bf16[48,1536]{1,0:T(8,128)(2,1)}, bf16[48,1536]{1,0:T(8,128)(2,1)S(1)}, u32[]{:S(2)}) copy-start(bf16[48,1536]{1,0:T(8,128)(2,1)S(1)} %collective-permute-done.9.refs_2_) | copy-start | bytes 442372
  81.7 12.0 %collective-permute-start.13 = (bf16[48,2304]{1,0:T(8,128)(2,1)S(1)}, bf16[48,2304]{1,0:T(8,128)(2,1)S(1)}, u32[]{:S(2)}, u32[]{:S(2)}) collective-permute-start(bf16[48,2304]{1,0:T(8,128)(2,1)S(1)} %pad_maximum_fusion.1), channel_id=1, source_target_pairs={{0,4},{2,6},{4,8},{6,10},{8,12},{10,14},{12,0},{14,2},{1,5},{3,7},... | collective-permute-start | bytes 663560 | tf_op jit(solution)/shard_map/ppermute | solution.py:25
  84.8 8.9 %copy-start.20 = (bf16[48,2304]{1,0:T(8,128)(2,1)}, bf16[48,2304]{1,0:T(8,128)(2,1)S(1)}, u32[]{:S(2)}) copy-start(bf16[48,2304]{1,0:T(8,128)(2,1)S(1)} %collective-permute-done.12.refs_5_) | copy-start | bytes 663556
  93.7 0.7 copy-start.21
  94.4 19.7 %copy-start.19 = (f32[48,128]{1,0:T(8,128)S(1)}, f32[48,128]{1,0:T(8,128)}, u32[]{:S(2)}) copy-start(f32[48,128]{1,0:T(8,128)} %get-tuple-element.86) | copy-start | bytes 73732
  99.7 21.3 %copy-start.11 = (f32[48,1408]{1,0:T(8,128)S(1)}, f32[48,1408]{1,0:T(8,128)}, u32[]{:S(2)}) copy-start(f32[48,1408]{1,0:T(8,128)} %get-tuple-element.85) | copy-start | bytes 811012
  99.8 8.6 %collective-permute-start.16 = (bf16[48,1408]{1,0:T(8,128)(2,1)S(1)}, bf16[48,1408]{1,0:T(8,128)(2,1)S(1)}, u32[]{:S(2)}, u32[]{:S(2)}) collective-permute-start(bf16[48,1408]{1,0:T(8,128)(2,1)S(1)} %get-tuple-element.80), channel_id=1, source_target_pairs={{0,2},{2,4},{4,6},{6,8},{8,10},{10,12},{12,14},{14,0},{1,3},{3,5},... | collective-permute-start | bytes 405512 | tf_op jit(solution)/shard_map/ppermute | solution.py:25
  99.8 7.5 %collective-permute-start.17 = (bf16[48,768]{1,0:T(8,128)(2,1)S(1)}, bf16[48,768]{1,0:T(8,128)(2,1)S(1)}, u32[]{:S(2)}, u32[]{:S(2)}) collective-permute-start(bf16[48,768]{1,0:T(8,128)(2,1)S(1)} %get-tuple-element.81), channel_id=1, source_target_pairs={{0,4},{2,6},{4,8},{6,10},{8,12},{10,14},{12,0},{14,2},{1,5},{3,7},... | collective-permute-start | bytes 221192 | tf_op jit(solution)/shard_map/ppermute | solution.py:25
  101.3 7.3 %collective-permute-start.20 = (bf16[48,640]{1,0:T(8,128)(2,1)S(1)}, bf16[48,640]{1,0:T(8,128)(2,1)S(1)}, u32[]{:S(2)}, u32[]{:S(2)}) collective-permute-start(bf16[48,640]{1,0:T(8,128)(2,1)S(1)} %get-tuple-element.84), channel_id=1, source_target_pairs={{0,12},{2,14},{4,0},{6,2},{8,4},{10,6},{12,8},{14,10},{1,13},{3,15... | collective-permute-start | bytes 184328 | tf_op jit(solution)/shard_map/ppermute | solution.py:25
  103.6 10.6 %collective-permute-start.14 = (bf16[48,1408]{1,0:T(8,128)(2,1)S(1)}, bf16[48,1408]{1,0:T(8,128)(2,1)S(1)}, u32[]{:S(2)}, u32[]{:S(2)}) collective-permute-start(bf16[48,1408]{1,0:T(8,128)(2,1)S(1)} %get-tuple-element.77), channel_id=1, source_target_pairs={{0,2},{2,4},{4,6},{6,8},{8,10},{10,12},{12,14},{14,0},{1,3},{3,5},... | collective-permute-start | bytes 405512 | tf_op jit(solution)/shard_map/ppermute | solution.py:25
  104.3 9.9 %collective-permute-start.15 = (bf16[48,1408]{1,0:T(8,128)(2,1)S(1)}, bf16[48,1408]{1,0:T(8,128)(2,1)S(1)}, u32[]{:S(2)}, u32[]{:S(2)}) collective-permute-start(bf16[48,1408]{1,0:T(8,128)(2,1)S(1)} %get-tuple-element.78), channel_id=1, source_target_pairs={{0,14},{2,0},{4,2},{6,4},{8,6},{10,8},{12,10},{14,12},{1,15},{3,1}... | collective-permute-start | bytes 405512 | tf_op jit(solution)/shard_map/ppermute | solution.py:25
  107.3 6.1 %collective-permute-start.19 = (bf16[48,1408]{1,0:T(8,128)(2,1)S(1)}, bf16[48,1408]{1,0:T(8,128)(2,1)S(1)}, u32[]{:S(2)}, u32[]{:S(2)}) collective-permute-start(bf16[48,1408]{1,0:T(8,128)(2,1)S(1)} %get-tuple-element.83), channel_id=1, source_target_pairs={{0,14},{2,0},{4,2},{6,4},{8,6},{10,8},{12,10},{14,12},{1,15},{3,1}... | collective-permute-start | bytes 405512 | tf_op jit(solution)/shard_map/ppermute | solution.py:25
  108.4 8.1 %collective-permute-start.18 = (bf16[48,1408]{1,0:T(8,128)(2,1)S(1)}, bf16[48,1408]{1,0:T(8,128)(2,1)S(1)}, u32[]{:S(2)}, u32[]{:S(2)}) collective-permute-start(bf16[48,1408]{1,0:T(8,128)(2,1)S(1)} %add_convert_fusion.1), channel_id=1, source_target_pairs={{0,4},{2,6},{4,8},{6,10},{8,12},{10,14},{12,0},{14,2},{1,5},{3,7},... | collective-permute-start | bytes 405512 | tf_op jit(solution)/shard_map/ppermute | solution.py:25
  113.4 27.5 %copy-start.7 = (f32[384,256]{1,0:T(8,128)S(1)}, f32[384,256]{1,0:T(8,128)}, u32[]{:S(2)}) copy-start(f32[384,256]{1,0:T(8,128)} %get-tuple-element.87.refs_11_) | copy-start | bytes 1179652
  113.5 27.5 %copy-start.2 = (bf16[384,3072]{1,0:T(8,128)(2,1)S(1)}, bf16[384,3072]{1,0:T(8,128)(2,1)}, u32[]{:S(2)}) copy-start(bf16[384,3072]{1,0:T(8,128)(2,1)} %refs_9_.1) | copy-start | bytes 7077892
  113.5 27.4 %copy-start.8 = (bf16[384,256]{1,0:T(8,128)(2,1)S(1)}, bf16[384,256]{1,0:T(8,128)(2,1)}, u32[]{:S(2)}) copy-start(bf16[384,256]{1,0:T(8,128)(2,1)} %get-tuple-element.88.refs_12_) | copy-start | bytes 589828
  113.5 7.5 %collective-permute-start.21 = (bf16[48,1408]{1,0:T(8,128)(2,1)S(1)}, bf16[48,1408]{1,0:T(8,128)(2,1)S(1)}, u32[]{:S(2)}, u32[]{:S(2)}) collective-permute-start(bf16[48,1408]{1,0:T(8,128)(2,1)S(1)} %add_convert_fusion), channel_id=1, source_target_pairs={{0,12},{2,14},{4,0},{6,2},{8,4},{10,6},{12,8},{14,10},{1,13},{3,15... | collective-permute-start | bytes 405512 | tf_op jit(solution)/shard_map/ppermute | solution.py:25
  121.4 6.3 %collective-permute-start.25 = (bf16[48,1408]{1,0:T(8,128)(2,1)S(1)}, bf16[48,1408]{1,0:T(8,128)(2,1)S(1)}, u32[]{:S(2)}, u32[]{:S(2)}) collective-permute-start(bf16[48,1408]{1,0:T(8,128)(2,1)S(1)} %multiply_convert_fusion.refs_0_), channel_id=1, source_target_pairs={{0,4},{2,6},{4,8},{6,10},{8,12},{10,14},{12,0},{14,2},{1,5},{3,7},... | collective-permute-start | bytes 405512 | tf_op jit(solution)/shard_map/ppermute | solution.py:25
  121.8 7.5 %collective-permute-start.24 = (bf16[48,1408]{1,0:T(8,128)(2,1)S(1)}, bf16[48,1408]{1,0:T(8,128)(2,1)S(1)}, u32[]{:S(2)}, u32[]{:S(2)}) collective-permute-start(bf16[48,1408]{1,0:T(8,128)(2,1)S(1)} %multiply_convert_fusion.refs_0_), channel_id=1, source_target_pairs={{0,12},{2,14},{4,0},{6,2},{8,4},{10,6},{12,8},{14,10},{1,13},{3,15... | collective-permute-start | bytes 405512 | tf_op jit(solution)/shard_map/ppermute | solution.py:25
  125.0 7.1 %collective-permute-start.23 = (bf16[48,1408]{1,0:T(8,128)(2,1)S(1)}, bf16[48,1408]{1,0:T(8,128)(2,1)S(1)}, u32[]{:S(2)}, u32[]{:S(2)}) collective-permute-start(bf16[48,1408]{1,0:T(8,128)(2,1)S(1)} %multiply_convert_fusion.refs_0_), channel_id=1, source_target_pairs={{0,2},{2,4},{4,6},{6,8},{8,10},{10,12},{12,14},{14,0},{1,3},{3,5},... | collective-permute-start | bytes 405512 | tf_op jit(solution)/shard_map/ppermute | solution.py:25
  125.0 10.4 %collective-permute-start.22 = (bf16[48,1408]{1,0:T(8,128)(2,1)S(1)}, bf16[48,1408]{1,0:T(8,128)(2,1)S(1)}, u32[]{:S(2)}, u32[]{:S(2)}) collective-permute-start(bf16[48,1408]{1,0:T(8,128)(2,1)S(1)} %multiply_convert_fusion.refs_0_), channel_id=1, source_target_pairs={{0,14},{2,0},{4,2},{6,4},{8,6},{10,8},{12,10},{14,12},{1,15},{3,1}... | collective-permute-start | bytes 405512 | tf_op jit(solution)/shard_map/ppermute | solution.py:25
  127.7 13.2 %collective-permute-start.27 = (bf16[48,1408]{1,0:T(8,128)(2,1)S(1)}, bf16[48,1408]{1,0:T(8,128)(2,1)S(1)}, u32[]{:S(2)}, u32[]{:S(2)}) collective-permute-start(bf16[48,1408]{1,0:T(8,128)(2,1)S(1)} %collective-permute-done.25.refs_4_), channel_id=1, source_target_pairs={{0,2},{2,4},{4,6},{6,8},{8,10},{10,12},{12,14},{14,0},{1,3},{3,5},... | collective-permute-start | bytes 405512 | tf_op jit(solution)/shard_map/ppermute | solution.py:25
  129.3 11.6 %collective-permute-start.26 = (bf16[48,1408]{1,0:T(8,128)(2,1)S(1)}, bf16[48,1408]{1,0:T(8,128)(2,1)S(1)}, u32[]{:S(2)}, u32[]{:S(2)}) collective-permute-start(bf16[48,1408]{1,0:T(8,128)(2,1)S(1)} %collective-permute-done.24.refs_3_), channel_id=1, source_target_pairs={{0,14},{2,0},{4,2},{6,4},{8,6},{10,8},{12,10},{14,12},{1,15},{3,1}... | collective-permute-start | bytes 405512 | tf_op jit(solution)/shard_map/ppermute | solution.py:25
  131.7 9.2 %collective-permute-start.28 = (bf16[48,768]{1,0:T(8,128)(2,1)S(1)}, bf16[48,768]{1,0:T(8,128)(2,1)S(1)}, u32[]{:S(2)}, u32[]{:S(2)}) collective-permute-start(bf16[48,768]{1,0:T(8,128)(2,1)S(1)} %slice.26), channel_id=1, source_target_pairs={{0,4},{2,6},{4,8},{6,10},{8,12},{10,14},{12,0},{14,2},{1,5},{3,7},... | collective-permute-start | bytes 221192 | tf_op jit(solution)/shard_map/ppermute | solution.py:25
  132.1 8.8 %collective-permute-start.29 = (bf16[48,640]{1,0:T(8,128)(2,1)S(1)}, bf16[48,640]{1,0:T(8,128)(2,1)S(1)}, u32[]{:S(2)}, u32[]{:S(2)}) collective-permute-start(bf16[48,640]{1,0:T(8,128)(2,1)S(1)} %slice.27), channel_id=1, source_target_pairs={{0,12},{2,14},{4,0},{6,2},{8,4},{10,6},{12,8},{14,10},{1,13},{3,15... | collective-permute-start | bytes 184328 | tf_op jit(solution)/shard_map/ppermute | solution.py:25
  141.0 15.0 %copy-start.4 = (bf16[3072,256]{1,0:T(8,128)(2,1)S(1)}, bf16[3072,256]{1,0:T(8,128)(2,1)}, u32[]{:S(2)}) copy-start(bf16[3072,256]{1,0:T(8,128)(2,1)} %w_in_ref.3) | copy-start | bytes 4718596
  145.7 13.0 %collective-permute-start.30 = (bf16[16,144,256]{2,1,0:T(8,128)(2,1)}, bf16[16,144,256]{2,1,0:T(8,128)(2,1)S(1)}, u32[]{:S(2)}, u32[]{:S(2)}) collective-permute-start(bf16[16,144,256]{2,1,0:T(8,128)(2,1)} %get-tuple-element.90), channel_id=1, source_target_pairs={{0,1},{1,0},{2,3},{3,2},{4,5},{5,4},{6,7},{7,6},{8,9},{9,8},{10,11... | collective-permute-start | bytes 3538952 | tf_op jit(solution)/shard_map/ppermute | solution.py:29
  155.9 2.8 %copy-start.6 = (bf16[16,144,256]{2,1,0:T(8,128)(2,1)S(1)}, bf16[16,144,256]{2,1,0:T(8,128)(2,1)}, u32[]{:S(2)}) copy-start(bf16[16,144,256]{2,1,0:T(8,128)(2,1)} %get-tuple-element.89.keep_ref) | copy-start | bytes 3538948
  201.0 4.9 %collective-permute-start.31 = (bf16[16,144,256]{2,1,0:T(8,128)(2,1)S(1)}, bf16[16,144,256]{2,1,0:T(8,128)(2,1)S(1)}, u32[]{:S(2)}, u32[]{:S(2)}) collective-permute-start(bf16[16,144,256]{2,1,0:T(8,128)(2,1)S(1)} %all_to_all.21.mine_ref), channel_id=1, source_target_pairs={{0,1},{1,0},{2,3},{3,2},{4,5},{5,4},{6,7},{7,6},{8,9},{9,8},{10,11... | collective-permute-start | bytes 3538952 | tf_op jit(solution)/shard_map/ppermute | solution.py:29
Sparse Core Ops, SparseCore 0:
  159.2 35.0 reduce-scatter.1
